TPU v7x, 32 devices: a whole 2x2x4 slice. The times are simulated.
32 devices in a mesh: groups: 2 (over y), branch: 2 (over core), dap: 4 (over z), tile: 2 (over x).
Axes of the slice: x: 2, y: 2, z: 4, core: 2. Of those that a mesh axis runs over, the one named last changes fastest.
Arguments:
- homolog_hidden: bfloat16 [64, 256, 256], P(('groups', 'dap'), ('branch', 'tile')), parts along dimension 0, may hold values from -6 to 6
- duo_hidden: bfloat16 [512, 256, 128], P(('groups', 'branch', 'tile'), 'dap'), parts along dimension 0, may hold values from -6 to 6
- homolog_valid_flags: int32 [64, 256], P(('groups', 'dap'), ('branch', 'tile')), parts along dimension 0, may hold values 0 or 1
- duo_valid_flags: int32 [512, 256], P(('groups', 'branch', 'tile'), 'dap'), parts along dimension 0, may hold values 0 or 1
- polymer_labeling: int32 [512], P('groups'), parts along dimension 0, may hold values from 0 to 3, never falling along the last dimension, each value on 1 to 128 neighbouring positions
- monomer_serials: int32 [512], P('groups'), parts along dimension 0, may hold values from 0 to 510, as said below
- separation_bin_vectors: bfloat16 [66, 128], replicated, may hold values from -4 to 4
- duo_logit_rescale: float32 [128], replicated, may hold values from 0.25 to 1.75
- duo_logit_projector: bfloat16 [128, 8], replicated, may hold values from -0.5 to 0.5
- homolog_heeded_rescale: float32 [256], replicated, may hold values from 0.25 to 1.75
- qkv_valve_projectors: bfloat16 [256, 1024], replicated
- heeded_exit_projector: bfloat16 [256, 256], replicated, may hold values from -0.375 to 0.375
- dyadic_rescale: float32 [256], replicated, may hold values from 0.25 to 1.75
- dyadic_factor_projector: bfloat16 [256, 64], replicated, may hold values from -0.375 to 0.375
- dyadic_exit_projector: bfloat16 [1024, 128], replicated, may hold values from -1.5 to 1.5
- triad_entry_rescales: float32 [2, 128], replicated, may hold values from 0.25 to 1.75
- triad_entry_projectors: bfloat16 [2, 128, 512], replicated, may hold values from -0.5 to 0.5
- triad_valve_projectors: bfloat16 [2, 128, 128], replicated, may hold values from -0.5 to 0.5
- triad_exit_rescales: float32 [2, 128], replicated, may hold values from 0.25 to 1.75
- triad_exit_projectors: bfloat16 [2, 128, 128], replicated, may hold values from -0.5 to 0.5
Outputs:
- lineup_updated_state: bfloat16 [64, 256, 256], P(('groups', 'dap'), ('branch', 'tile')), parts along dimension 0
- pair_out: bfloat16 [512, 256, 128], P(('groups', 'branch', 'tile'), 'dap'), parts along dimension 0
There are 2 independent parts, one for each index of `groups`. A program takes and returns all parts, laid end to end along the dimension named above; an argument that names none is the same for every part. Nothing has to cross between parts.
Inputs may be any that keep to these rules, and one draw needn't show every extreme that they name: `monomer_serials`: starts at 0 and rises by 1 to 3 from each residue to the next. `polymer_labeling`: chains are contiguous runs of 1 to 128 residues, numbered in order.
All inputs are finite; a program needn't handle non-finite values. No bound on the sum of `homolog_valid_flags` or of `duo_valid_flags` on one device may be relied on, other than what follows from the above.
Results may differ from a plain program's by a relative error of at most 0.015.
Values may be sent and summed in bfloat16 or wider, within the bound.
A program may use at most 128 MiB of HBM per device.

v0:
```python
import jax
import jax.numpy as jnp
from jax import lax
from jax.sharding import PartitionSpec as P

REL_BINS = 66


norm_eps = 1e-05
mask_big = 1000000000.0
count_eps = 0.001


def standardize_features(values, norm_gain, norm_axis):
    values = values.astype(jnp.float32)
    mean_val = jnp.mean(values, axis=norm_axis, keepdims=True)
    centred = values - mean_val
    spread = jnp.mean(centred * centred, axis=norm_axis, keepdims=True)
    return centred * lax.rsqrt(spread + norm_eps) * norm_gain


def threeway_update(
    duo_hidden_values, duo_valid_flags, norm_gain, w_in, w_gate, out_gain, w_out, incoming
):
    width_tri = w_in.shape[1] // 4
    tri_normed = standardize_features(duo_hidden_values, norm_gain, 2).astype(jnp.bfloat16)
    mapped_contents = jnp.einsum(
        "ijc,cd->idj", tri_normed, w_in, preferred_element_type=jnp.float32
    )
    mask_as_float = duo_valid_flags.astype(jnp.float32)[:, None, :]
    left_fac = (
        jax.nn.sigmoid(mapped_contents[:, width_tri : 2 * width_tri])
        * mapped_contents[:, :width_tri]
        * mask_as_float
    ).astype(jnp.bfloat16)
    right_fac = (
        jax.nn.sigmoid(mapped_contents[:, 3 * width_tri :])
        * mapped_contents[:, 2 * width_tri : 3 * width_tri]
        * mask_as_float
    ).astype(jnp.bfloat16)
    sigmoid_switches = jax.nn.sigmoid(
        jnp.einsum("ijc,cd->ijd", tri_normed, w_gate, preferred_element_type=jnp.float32)
    )
    left_split, right_split = (
        lax.all_to_all(left_fac, "dap", split_axis=1, concat_axis=2, tiled=True),
        lax.all_to_all(right_fac, "dap", split_axis=1, concat_axis=2, tiled=True),
    )
    if not incoming:
        product = jnp.einsum(
            "ick,jck->icj",
            left_split,
            lax.all_gather(right_split, ("branch", "tile"), axis=0, tiled=True),
            preferred_element_type=jnp.float32,
        )
    else:
        product = lax.psum_scatter(
            jnp.einsum(
                "kci,kcj->icj", left_split, right_split, preferred_element_type=jnp.float32
            ).astype(jnp.bfloat16),
            ("branch", "tile"),
            scatter_dimension=0,
            tiled=True,
        ).astype(jnp.float32)
    merged = lax.all_to_all(
        product.astype(jnp.bfloat16), "dap", split_axis=2, concat_axis=1, tiled=True
    )
    product_normed = standardize_features(merged, out_gain[:, None], 1).astype(jnp.bfloat16)
    update = jnp.einsum("icj,cz->ijz", product_normed, w_out, preferred_element_type=jnp.float32)
    return duo_hidden_values + sigmoid_switches * update


def body(
    homolog_hidden,
    duo_hidden,
    homolog_valid_flags,
    duo_valid_flags,
    polymer_labeling,
    monomer_serials,
    separation_bin_vectors,
    duo_logit_rescale,
    duo_logit_projector,
    homolog_heeded_rescale,
    qkv_valve_projectors,
    heeded_exit_projector,
    dyadic_rescale,
    dyadic_factor_projector,
    dyadic_exit_projector,
    triad_entry_rescales,
    triad_entry_projectors,
    triad_valve_projectors,
    triad_exit_rescales,
    triad_exit_projectors,
):
    lines_each_shard, sites_each_shard, lineup_feature_extent = homolog_hidden.shape
    columns_per_device = duo_hidden.shape[1]
    number_of_heads = duo_logit_projector.shape[1]
    head_channels = lineup_feature_extent // number_of_heads
    outer_channels = dyadic_factor_projector.shape[1] // 2
    row_start = lax.axis_index(("branch", "tile")) * sites_each_shard
    col_start = lax.axis_index("dap") * columns_per_device
    rel_reach = (REL_BINS - 2) // 2
    res_rows = lax.dynamic_slice_in_dim(monomer_serials, row_start, sites_each_shard)
    res_cols = lax.dynamic_slice_in_dim(monomer_serials, col_start, columns_per_device)
    chain_rows = lax.dynamic_slice_in_dim(polymer_labeling, row_start, sites_each_shard)
    chain_cols = lax.dynamic_slice_in_dim(polymer_labeling, col_start, columns_per_device)
    offset = jnp.clip(res_rows[:, None] - res_cols[None, :], -rel_reach, rel_reach) + rel_reach
    rel_bins = jnp.where(chain_rows[:, None] == chain_cols[None, :], offset, REL_BINS - 1)
    one_hot = (rel_bins[:, :, None] == jnp.arange(REL_BINS, dtype=jnp.int32)[None, None, :]).astype(
        jnp.bfloat16
    )
    duo_hidden_values = duo_hidden.astype(jnp.float32) + jnp.einsum(
        "ijb,bc->ijc", one_hot, separation_bin_vectors, preferred_element_type=jnp.float32
    )
    pair_normed = standardize_features(duo_hidden_values, duo_logit_rescale, 2).astype(jnp.bfloat16)
    local_bias = jnp.einsum(
        "ijc,ch->hij", pair_normed, duo_logit_projector, preferred_element_type=jnp.float32
    ).astype(jnp.bfloat16)
    row_bias = lax.all_gather(local_bias, "dap", axis=2, tiled=True)
    lineup_standardized = standardize_features(homolog_hidden, homolog_heeded_rescale, 2).astype(
        jnp.bfloat16
    )
    mapped_contents = jnp.einsum(
        "ezp,pb->ezb", lineup_standardized, qkv_valve_projectors, preferred_element_type=jnp.float32
    )
    asking_array = (mapped_contents[..., :lineup_feature_extent] * head_channels ** (-0.5)).astype(
        jnp.bfloat16
    )
    asking_array = asking_array.reshape(
        lines_each_shard, sites_each_shard, number_of_heads, head_channels
    )
    key_value_pairs = mapped_contents[
        ..., lineup_feature_extent : 3 * lineup_feature_extent
    ].astype(jnp.bfloat16)
    sigmoid_switches = jax.nn.sigmoid(mapped_contents[..., 3 * lineup_feature_extent :])
    mask_as_float = homolog_valid_flags.astype(jnp.bfloat16)
    run_max = jnp.full((lines_each_shard, number_of_heads, sites_each_shard), -jnp.inf, jnp.float32)
    run_sum = jnp.zeros((lines_each_shard, number_of_heads, sites_each_shard), jnp.float32)
    run_acc = jnp.zeros(
        (lines_each_shard, number_of_heads, sites_each_shard, head_channels), jnp.float32
    )
    key_value_slice = lax.all_gather(key_value_pairs, ("branch", "tile"), axis=1, tiled=True)
    mask_piece = lax.all_gather(mask_as_float, ("branch", "tile"), axis=1, tiled=True)
    slice_length = key_value_slice.shape[1]
    key_per_head = key_value_slice[..., :lineup_feature_extent].reshape(
        lines_each_shard, slice_length, number_of_heads, head_channels
    )
    value_per_head = key_value_slice[..., lineup_feature_extent:].reshape(
        lines_each_shard, slice_length, number_of_heads, head_channels
    )
    key_bias = row_bias.astype(jnp.float32)
    scores = jnp.einsum(
        "sihd,sjhd->shij", asking_array, key_per_head, preferred_element_type=jnp.float32
    )
    scores = (
        scores
        + key_bias[None]
        + ((mask_piece.astype(jnp.float32) - 1.0) * mask_big)[:, None, None, :]
    )
    new_max = jnp.max(scores, axis=-1)
    old_scale = jnp.exp(run_max - new_max)
    weights = jnp.exp(scores - new_max[..., None])
    run_sum = run_sum * old_scale + jnp.sum(weights, axis=-1)
    run_acc = run_acc * old_scale[..., None] + jnp.einsum(
        "shij,sjhd->shid",
        weights.astype(jnp.bfloat16),
        value_per_head,
        preferred_element_type=jnp.float32,
    )
    run_max, run_sum, run_acc = (new_max, run_sum, run_acc)
    focused_readout = run_acc / run_sum[..., None]
    focused_readout = jnp.transpose(focused_readout, (0, 2, 1, 3)).reshape(
        lines_each_shard, sites_each_shard, lineup_feature_extent
    )
    merged_focus_groups = (sigmoid_switches * focused_readout).astype(jnp.bfloat16)
    lineup_updated_state = (
        homolog_hidden.astype(jnp.float32)
        + jnp.einsum(
            "ezp,pb->ezb",
            merged_focus_groups,
            heeded_exit_projector,
            preferred_element_type=jnp.float32,
        )
    ).astype(jnp.bfloat16)
    outer_product_normalized = standardize_features(lineup_updated_state, dyadic_rescale, 2).astype(
        jnp.bfloat16
    )
    factors = (
        jnp.einsum(
            "ezp,pb->ezb",
            outer_product_normalized,
            dyadic_factor_projector,
            preferred_element_type=jnp.float32,
        )
        * homolog_valid_flags.astype(jnp.float32)[..., None]
    )
    left_flat = (
        factors[..., :outer_channels]
        .astype(jnp.bfloat16)
        .reshape(lines_each_shard, sites_each_shard * outer_channels)
    )
    right_flat = (
        factors[..., outer_channels:]
        .astype(jnp.bfloat16)
        .reshape(lines_each_shard, sites_each_shard * outer_channels)
    )
    right_all, mask_all = (
        lax.all_gather(right_flat, ("branch", "tile"), axis=1, tiled=True),
        lax.all_gather(mask_as_float, ("branch", "tile"), axis=1, tiled=True),
    )
    total_res = mask_all.shape[1]
    right_all = right_all.reshape(lines_each_shard, total_res, outer_channels)
    right_factor_rows, mask_right = (
        lax.all_to_all(right_all, "dap", split_axis=1, concat_axis=0, tiled=True),
        lax.all_to_all(mask_all, "dap", split_axis=1, concat_axis=0, tiled=True),
    )
    left_factor_rows, mask_rows = (
        lax.all_gather(left_flat, "dap", axis=0, tiled=True),
        lax.all_gather(mask_as_float, "dap", axis=0, tiled=True),
    )
    alignment_rows = left_factor_rows.shape[0]
    left_factor_rows = left_factor_rows.reshape(alignment_rows, sites_each_shard, outer_channels)
    counts = jnp.einsum("si,sj->ij", mask_rows, mask_right, preferred_element_type=jnp.float32)
    outer_prod = jnp.einsum(
        "sic,sjd->ijcd", left_factor_rows, right_factor_rows, preferred_element_type=jnp.float32
    ).astype(jnp.bfloat16)
    outer_prod = outer_prod.reshape(
        sites_each_shard, columns_per_device, outer_channels * outer_channels
    )
    update = jnp.einsum(
        "ijk,kz->ijz", outer_prod, dyadic_exit_projector, preferred_element_type=jnp.float32
    )
    duo_hidden_values = duo_hidden_values + update / (count_eps + counts)[..., None]
    for threefold_module in range(2):
        duo_hidden_values = threeway_update(
            duo_hidden_values,
            duo_valid_flags,
            triad_entry_rescales[threefold_module],
            triad_entry_projectors[threefold_module],
            triad_valve_projectors[threefold_module],
            triad_exit_rescales[threefold_module],
            triad_exit_projectors[threefold_module],
            threefold_module == 1,
        )
    return (lineup_updated_state, duo_hidden_values.astype(jnp.bfloat16))


def solution(mesh):
    placed = (
        P(("groups", "dap"), ("branch", "tile"), None),
        P(("groups", "branch", "tile"), "dap", None),
        P(("groups", "dap"), ("branch", "tile")),
        P(("groups", "branch", "tile"), "dap"),
        P("groups"),
        P("groups"),
        P(),
        P(),
        P(),
        P(),
        P(),
        P(),
        P(),
        P(),
        P(),
        P(),
        P(),
        P(),
        P(),
        P(),
    )
    return jax.shard_map(
        body,
        mesh=mesh,
        in_specs=placed,
        out_specs=(
            P(("groups", "dap"), ("branch", "tile"), None),
            P(("groups", "branch", "tile"), "dap", None),
        ),
        check_vma=False,
    )
```

profile of v0, /device:TPU:0, one launch (start us, length us, event | category | flops | bytes accessed | tf_op | source)
XLA Modules:
  0.0 520.1 jit_solution(10348748463445735819)
XLA Ops:
  13.4 9.0 %all-gather = bf16[4,64,8]{1,2,0:T(8,128)(2,1)S(1)} all-gather(bf16[1,64,8]{1,2,0:T(8,128)(2,1)S(1)} %bitcast.206), channel_id=1, replica_groups=mesh['groups'=2,'branch'=2,'dap'=4,'tile'=2] {'branch','tile'}, dimensions={0}, use_global_device_ids=true | all-gather | bytes 5120 | tf_op jit(solution)/shard_map/all_gather | solution.py:142
  23.3 5.1 all-to-all-start.1
  35.6 16.7 %all_gather.23 = bf16[8,64,256]{1,0,2:T(8,128)(2,1)S(1)} all-gather(bf16[8,64,64]{1,0,2:T(8,128)(2,1)S(1)} %copy.100), channel_id=1, replica_groups=mesh['groups'=2,'branch'=2,'dap'=4,'tile'=2] {'dap'}, dimensions={2}, use_global_device_ids=true | all-gather | bytes 327680 | tf_op jit(solution)/shard_map/all_gather | solution.py:118
  52.9 11.9 %all_gather.27 = bf16[32,64]{1,0:T(8,128)(2,1)S(1)} all-gather(bf16[8,64]{1,0:T(8,128)(2,1)S(1)} %get-tuple-element.13), channel_id=1, replica_groups=mesh['groups'=2,'branch'=2,'dap'=4,'tile'=2] {'dap'}, dimensions={0}, use_global_device_ids=true | all-gather | bytes 5120 | tf_op jit(solution)/shard_map/all_gather | solution.py:218
  76.9 4.8 fusion.39
  85.6 9.8 %all_gather.25 = bf16[8,8192]{1,0:T(8,128)(2,1)S(1)} all-gather(bf16[8,2048]{1,0:T(8,128)(2,1)S(1)} %reshape.212), channel_id=1, replica_groups=mesh['groups'=2,'branch'=2,'dap'=4,'tile'=2] {'branch','tile'}, dimensions={1}, use_global_device_ids=true | all-gather | bytes 163840 | tf_op jit(solution)/shard_map/all_gather | solution.py:207
  101.4 14.1 %all_gather.26 = bf16[32,2048]{1,0:T(8,128)(2,1)S(1)} all-gather(bf16[8,2048]{1,0:T(8,128)(2,1)S(1)} %reshape.214), channel_id=1, replica_groups=mesh['groups'=2,'branch'=2,'dap'=4,'tile'=2] {'dap'}, dimensions={0}, use_global_device_ids=true | all-gather | bytes 163840 | tf_op jit(solution)/shard_map/all_gather | solution.py:217
  117.0 8.1 %convert_bitcast_fusion = bf16[64,64,32,32]{0,1,2,3:T(8,128)(2,1)} fusion(bf16[32,64,32]{1,0,2:T(8,128)(2,1)S(1)} %copy.110, bf16[4,8,64,32]{2,0,3,1:T(4,128)(2,1)S(1)} %bitcast.201), kind=kOutput, calls=%fused_computation | convolution fusion | flops 272629760 | bytes 8650752 | tf_op jit(solution)/shard_map/sic,sjd->ijcd/dot_general | solution.py:223
  125.1 23.6 %copy.111 = bf16[64,64,32,32]{1,3,2,0:T(8,128)(2,1)} copy(bf16[64,64,32,32]{0,1,2,3:T(8,128)(2,1)} %convert_bitcast_fusion) | data formatting | bytes 16777216 | tf_op jit(solution)/shard_map/convert_element_type | solution.py:225
  148.7 9.0 %fusion.103 = (f32[64,64]{1,0:T(8,128)S(1)}, f32[64,64,128]{2,1,0:T(8,128)S(1)}) fusion(f32[64,64,128]{2,1,0:T(8,128)S(1)} %get-tuple-element.21, f32[64,64]{1,0:T(8,128)S(1)} %convolution_add_fusion.1, bf16[64,64,1024]{1,2,0:T(8,128)(2,1)} %bitcast.182, bf16[1024,128]{1,0:T(8,128)(2,1)S(1)} %copy-done.26), kind=kOutput, calls=%fused_computation.160 | convolution fusion | flops 1075310592 | bytes 12877824 | tf_op jit(solution)/shard_map/ijk,kz->ijz/dot_general | solution.py:229
  169.3 28.6 %all_to_all.127 = bf16[4,2,65536]{2,1,0:T(2,128)(2,1)} all-to-all(bf16[4,2,65536]{2,1,0:T(2,128)(2,1)} %reshape.251), channel_id=1, replica_groups=mesh['groups'=2,'branch'=2,'dap'=4,'tile'=2] {'dap'}, dimensions={0} | all-to-all | bytes 2097152 | tf_op jit(solution)/shard_map/all_to_all | solution.py:46
  204.3 4.4 all_to_all.104
  215.3 28.4 %all_to_all.128 = bf16[4,2,65536]{2,1,0:T(2,128)(2,1)} all-to-all(bf16[4,2,65536]{2,1,0:T(2,128)(2,1)} %reshape.253), channel_id=1, replica_groups=mesh['groups'=2,'branch'=2,'dap'=4,'tile'=2] {'dap'}, dimensions={0} | all-to-all | bytes 2097152 | tf_op jit(solution)/shard_map/all_to_all | solution.py:45
  261.1 4.5 reshape.255
  265.6 4.4 all-to-all-start.4
  272.6 22.0 %all-to-all-done.4 = bf16[4,2,65536]{2,1,0:T(2,128)(2,1)} async-done(((bf16[4,2,65536]{2,1,0:T(2,128)(2,1)}), bf16[4,2,65536]{2,1,0:T(2,128)(2,1)}, u32[]{:S(2)}, u32[]{:S(2)}) %all-to-all-start.4) | async-done | bytes 1048608 | tf_op jit(solution)/shard_map/all_to_all | solution.py:64
  297.8 5.1 copy.121
  315.5 4.7 copy.123
  320.2 4.4 reshape.257
  328.8 4.8 copy.126
  337.9 16.2 %all-to-all-done.5 = bf16[4,2,65536]{2,1,0:T(2,128)(2,1)} async-done(((bf16[4,2,65536]{2,1,0:T(2,128)(2,1)}), bf16[4,2,65536]{2,1,0:T(2,128)(2,1)}, u32[]{:S(2)}, u32[]{:S(2)}) %all-to-all-start.5) | async-done | bytes 1048608 | tf_op jit(solution)/shard_map/all_to_all | solution.py:46
  363.0 4.9 copy.125
  372.1 11.5 %all-to-all-done.6 = bf16[4,2,65536]{2,1,0:T(2,128)(2,1)} async-done(((bf16[4,2,65536]{2,1,0:T(2,128)(2,1)}), bf16[4,2,65536]{2,1,0:T(2,128)(2,1)}, u32[]{:S(2)}, u32[]{:S(2)}) %all-to-all-start.6) | async-done | bytes 1048608 | tf_op jit(solution)/shard_map/all_to_all | solution.py:45
  388.0 4.9 copy.128
  397.2 4.8 convert_bitcast_fusion.1
  401.9 7.9 %copy.129 = bf16[256,32,256]{2,1,0:T(8,128)(2,1)} copy(bf16[256,32,256]{0,2,1:T(8,128)(2,1)} %convert_bitcast_fusion.1) | data formatting | bytes 8388608 | tf_op jit(solution)/shard_map/convert_element_type | solution.py:59
  409.9 44.2 %reduce-scatter.2.cloned.1.call-done = bf16[64,32,256]{2,1,0:T(8,128)(2,1)} async-done(((bf16[256,32,256]{2,1,0:T(8,128)(2,1)}), bf16[64,32,256]{2,1,0:T(8,128)(2,1)}) %reduce-scatter.2.cloned.1.call-update) | async-done | bytes 1048592 | tf_op jit(solution)/shard_map/reduce_scatter | solution.py:56
  454.1 5.4 %copy.130 = bf16[64,32,256]{0,1,2:T(8,128)(2,1)} copy(bf16[64,32,256]{2,1,0:T(8,128)(2,1)} %reduce-scatter.2.cloned.1.call-done) | data formatting | bytes 2097152 | tf_op jit(solution)/shard_map/reduce_scatter | solution.py:56
  459.6 4.4 reshape.261
  463.9 4.8 all-to-all-start.7
  471.4 23.2 %all-to-all-done.7 = bf16[4,2,65536]{2,1,0:T(2,128)(2,1)} async-done(((bf16[4,2,65536]{2,1,0:T(2,128)(2,1)}), bf16[4,2,65536]{2,1,0:T(2,128)(2,1)}, u32[]{:S(2)}, u32[]{:S(2)}) %all-to-all-start.7) | async-done | bytes 1048608 | tf_op jit(solution)/shard_map/all_to_all | solution.py:64
  498.9 6.6 %copy.131 = f32[64,32,4,64]{3,1,2,0:T(8,128)} copy(bf16[64,32,4,64]{0,1,3,2:T(8,128)(2,1)} %bitcast.184) | data formatting | bytes 3145728 | tf_op jit(solution)/shard_map/convert_element_type | solution.py:15
  (174 shorter events, 142.9 us)
Async XLA Ops:
  7.2 2.5 copy-start
  7.2 57.7 %all-gather.4.cloned.1.call-start = ((), (), s32[]{:S(2)}) async-start(), calls=%async_computation.9 | async-start | bytes 2621440 | tf_op jit(solution)/shard_map/all_gather | solution.py:141
  9.6 3.7 copy-start.19
  9.6 18.7 %copy-start.21 = (s32[256]{0:T(256)S(1)}, s32[256]{0:T(256)}, u32[]{:S(2)}) copy-start(s32[256]{0:T(256)} %param.24) | copy-start | bytes 3076
  9.6 18.7 %copy-start.22 = (s32[256]{0:T(256)S(1)}, s32[256]{0:T(256)}, u32[]{:S(2)}) copy-start(s32[256]{0:T(256)} %param.25) | copy-start | bytes 3076
  9.7 18.9 %copy-start.16 = (bf16[66,128]{1,0:T(8,128)(2,1)S(1)}, bf16[66,128]{1,0:T(8,128)(2,1)}, u32[]{:S(2)}) copy-start(bf16[66,128]{1,0:T(8,128)(2,1)} %param.26) | copy-start | bytes 50692
  23.3 41.5 %all-to-all-start.1 = ((bf16[4,2,256]{2,1,0:T(2,128)(2,1)}), bf16[4,2,256]{2,1,0:T(2,128)(2,1)S(1)}, u32[]{:S(2)}, u32[]{:S(2)}) async-start(bf16[4,2,256]{2,1,0:T(2,128)(2,1)} %reshape.249), calls=%async_computation.1 | async-start | bytes 8192 | tf_op jit(solution)/shard_map/all_to_all | solution.py:214
  28.5 3.7 copy-start.20
  28.5 3.7 copy-start.25
  30.9 3.0 copy-start.23
  33.8 19.1 %copy-start.15 = (s32[64,64]{1,0:T(8,128)S(1)}, s32[64,64]{1,0:T(8,128)}, u32[]{:S(2)}) copy-start(s32[64,64]{1,0:T(8,128)} %param.23) | copy-start | bytes 49156
  76.9 6.3 %copy-start.9 = (bf16[8,64,256]{2,1,0:T(8,128)(2,1)S(1)}, bf16[8,64,256]{2,1,0:T(8,128)(2,1)}, u32[]{:S(2)}) copy-start(bf16[8,64,256]{2,1,0:T(8,128)(2,1)} %param.20) | copy-start | bytes 786436
  76.9 6.4 %copy-start.27 = (bf16[256,256]{1,0:T(8,128)(2,1)S(1)}, bf16[256,256]{1,0:T(8,128)(2,1)}, u32[]{:S(2)}) copy-start(bf16[256,256]{1,0:T(8,128)(2,1)} %param.31) | copy-start | bytes 393220
  81.7 3.3 copy-start.29
  81.7 3.3 copy-start.30
  84.6 12.7 %copy-start.13 = (bf16[8,64,256]{2,1,0:T(8,128)(2,1)}, bf16[8,64,256]{2,1,0:T(8,128)(2,1)S(1)}, u32[]{:S(2)}) copy-start(bf16[8,64,256]{2,1,0:T(8,128)(2,1)S(1)} %get-tuple-element.25) | copy-start | bytes 786436
  97.3 19.0 %all-to-all-start = ((bf16[4,2,8192]{2,1,0:T(2,128)(2,1)}), bf16[4,2,8192]{2,1,0:T(2,128)(2,1)S(1)}, u32[]{:S(2)}, u32[]{:S(2)}) async-start(bf16[4,2,8192]{2,1,0:T(2,128)(2,1)} %reshape.247), calls=%async_computation | async-start | bytes 262144 | tf_op jit(solution)/shard_map/all_to_all | solution.py:213
  100.9 152.8 %all-gather.6.cloned.1.call-start = ((), (), s32[]{:S(2)}) async-start(), calls=%async_computation.10 | async-start | bytes 5242880 | tf_op jit(solution)/shard_map/all_gather | solution.py:52
  125.1 23.6 %copy-start.26 = (bf16[1024,128]{1,0:T(8,128)(2,1)S(1)}, bf16[1024,128]{1,0:T(8,128)(2,1)}, u32[]{:S(2)}) copy-start(bf16[1024,128]{1,0:T(8,128)(2,1)} %param.34) | copy-start | bytes 786436
  157.8 2.7 copy-start.4
  261.1 8.9 %copy-start.24 = (f32[2,128]{1,0:T(2,128)S(1)}, f32[2,128]{1,0:T(2,128)}, u32[]{:S(2)}) copy-start(f32[2,128]{1,0:T(2,128)} %param.38) | copy-start | bytes 3076
  261.1 9.0 %copy-start.5 = (f32[64,64,128]{2,1,0:T(8,128)S(1)}, f32[64,64,128]{2,1,0:T(8,128)}, u32[]{:S(2)}) copy-start(f32[64,64,128]{2,1,0:T(8,128)} %copy-done.4) | copy-start | bytes 6291460
  261.1 9.0 %copy-start.14 = (bf16[2,128,128]{2,1,0:T(8,128)(2,1)S(1)}, bf16[2,128,128]{2,1,0:T(8,128)(2,1)}, u32[]{:S(2)}) copy-start(bf16[2,128,128]{2,1,0:T(8,128)(2,1)} %param.37) | copy-start | bytes 196612
  265.6 29.0 %all-to-all-start.4 = ((bf16[4,2,65536]{2,1,0:T(2,128)(2,1)}), bf16[4,2,65536]{2,1,0:T(2,128)(2,1)}, u32[]{:S(2)}, u32[]{:S(2)}) async-start(bf16[4,2,65536]{2,1,0:T(2,128)(2,1)} %reshape.255), calls=%async_computation.4 | async-start | bytes 2097152 | tf_op jit(solution)/shard_map/all_to_all | solution.py:64
  302.9 3.4 copy-start.2
  307.2 2.2 copy-start.10
  307.2 2.2 copy-start.28
  324.6 29.5 %all-to-all-start.5 = ((bf16[4,2,65536]{2,1,0:T(2,128)(2,1)}), bf16[4,2,65536]{2,1,0:T(2,128)(2,1)}, u32[]{:S(2)}, u32[]{:S(2)}) async-start(bf16[4,2,65536]{2,1,0:T(2,128)(2,1)} %reshape.257), calls=%async_computation.5 | async-start | bytes 2097152 | tf_op jit(solution)/shard_map/all_to_all | solution.py:46
  354.1 29.6 %all-to-all-start.6 = ((bf16[4,2,65536]{2,1,0:T(2,128)(2,1)}), bf16[4,2,65536]{2,1,0:T(2,128)(2,1)}, u32[]{:S(2)}, u32[]{:S(2)}) async-start(bf16[4,2,65536]{2,1,0:T(2,128)(2,1)} %reshape.259), calls=%async_computation.6 | async-start | bytes 2097152 | tf_op jit(solution)/shard_map/all_to_all | solution.py:45
  358.4 95.7 %reduce-scatter.2.cloned.1.call-start = ((), (), s32[]{:S(2)}) async-start(), calls=%async_computation.11 | async-start | bytes 5242880 | tf_op jit(solution)/shard_map/reduce_scatter | solution.py:56
  463.9 30.7 %all-to-all-start.7 = ((bf16[4,2,65536]{2,1,0:T(2,128)(2,1)}), bf16[4,2,65536]{2,1,0:T(2,128)(2,1)}, u32[]{:S(2)}, u32[]{:S(2)}) async-start(bf16[4,2,65536]{2,1,0:T(2,128)(2,1)} %reshape.261), calls=%async_computation.8 | async-start | bytes 2097152 | tf_op jit(solution)/shard_map/all_to_all | solution.py:64
  505.5 3.4 copy-start.3
  (8 other events, 12.3 us)
Sparse Core Ops, SparseCore 0:
  13.5 25.2 all-gather.3
  208.9 34.0 all-gather.5
  410.0 44.0 reduce-scatter.1
where the time goes:
time: 530 us; the launch traced here: 520 us
  local copies, waits for them, and re-layouts  169 us (32%)
  blocking collectives  119 us (22%)
  waiting for transfers between devices  117 us (22%)
  matrix products  50.5 us (10%)
  starting transfers between devices  26.7 us (5%)
  other arithmetic  23.4 us (4%)
  between operations  15 us (3%)
    unnamed x79, local copies, waits for them, and re-layouts  51.9 us
    all_to_all x2, waiting for transfers between devices, threeway_update(): lax.all_to_all(product.astype(jnp.bfloat16), 'dap', split_axis=2, concat_...  45.2 us
    reduce_scatter x1, waiting for transfers between devices, threeway_update(): lax.psum_scatter(jnp.einsum('kci,kcj->icj', left_split, right_split, pref...  44.2 us
    all_to_all x1, blocking collectives, threeway_update(): lax.all_to_all(right_fac, 'dap', split_axis=1, concat_axis=2, tiled=True)  28.6 us
    all_to_all x1, blocking collectives, threeway_update(): lax.all_to_all(left_fac, 'dap', split_axis=1, concat_axis=2, tiled=True)  28.4 us
    convert_element_type x1, local copies, waits for them, and re-layouts, body(): outer_prod = jnp.einsum('sic,sjd->ijcd', left_factor_rows, right_factor_r...  23.6 us
    all_to_all x4, local copies, waits for them, and re-layouts, threeway_update(): lax.all_to_all(right_fac, 'dap', split_axis=1, concat_axis=2, tiled=True)  16.8 us
    all_gather x1, blocking collectives, body(): row_bias = lax.all_gather(local_bias, 'dap', axis=2, tiled=True)  16.7 us
  transfers between devices with their start and end apart: 9, of which 5 were waited for; matrix products, arithmetic and copies ran while one was open for 9% of the time, Pallas kernels for 0%

commit v1 on v0

--- a/solution.py
+++ b/solution.py
@@ -23,50 +23,61 @@
     duo_hidden_values, duo_valid_flags, norm_gain, w_in, w_gate, out_gain, w_out, incoming
 ):
     width_tri = w_in.shape[1] // 4
+    rows, cols = duo_valid_flags.shape
     tri_normed = standardize_features(duo_hidden_values, norm_gain, 2).astype(jnp.bfloat16)
-    mapped_contents = jnp.einsum(
-        "ijc,cd->idj", tri_normed, w_in, preferred_element_type=jnp.float32
-    )
-    mask_as_float = duo_valid_flags.astype(jnp.float32)[:, None, :]
-    left_fac = (
-        jax.nn.sigmoid(mapped_contents[:, width_tri : 2 * width_tri])
-        * mapped_contents[:, :width_tri]
-        * mask_as_float
-    ).astype(jnp.bfloat16)
-    right_fac = (
-        jax.nn.sigmoid(mapped_contents[:, 3 * width_tri :])
-        * mapped_contents[:, 2 * width_tri : 3 * width_tri]
-        * mask_as_float
-    ).astype(jnp.bfloat16)
+    flags = duo_valid_flags.astype(jnp.float32)
+    if incoming:
+        positions = jnp.transpose(tri_normed, (1, 0, 2))
+        flags = flags.T
+        share_axis, spread_axis = ("branch", "tile"), "dap"
+        kept, summed = cols, rows
+    else:
+        positions = tri_normed
+        share_axis, spread_axis = "dap", ("branch", "tile")
+        kept, summed = rows, cols
+    positions = positions.reshape(kept * summed, width_tri)
+    flags = flags.reshape(1, kept * summed)
+    shares = lax.axis_size(share_axis)
+    share = width_tri // shares
+    mapped = jnp.einsum("pc,cd->dp", positions, w_in, preferred_element_type=jnp.float32)
+    blocks = [mapped[n * width_tri : (n + 1) * width_tri] for n in range(4)]
+    left_fac = (jax.nn.sigmoid(blocks[1]) * blocks[0] * flags).astype(jnp.bfloat16)
+    right_fac = (jax.nn.sigmoid(blocks[3]) * blocks[2] * flags).astype(jnp.bfloat16)
+
+    def by_channel_share(factor):
+        got = lax.all_to_all(
+            factor.reshape(shares, share, kept * summed), share_axis, split_axis=0, concat_axis=0
+        )
+        got = got.reshape(shares, share, kept, summed)
+        return jnp.transpose(got, (1, 2, 0, 3)).reshape(share, kept, shares * summed)
+
+    if incoming:
+        left_own = by_channel_share(left_fac)
+        left_all = lax.all_gather(left_own, spread_axis, axis=0)
+        right_own = by_channel_share(right_fac)
+        product = jnp.einsum(
+            "gcik,cjk->gicj", left_all, right_own, preferred_element_type=jnp.float32
+        ).astype(jnp.bfloat16)
+        product = product.reshape(shares, rows, share, cols)
+        product = jnp.transpose(product, (0, 2, 1, 3))
+    else:
+        right_own = by_channel_share(right_fac)
+        right_all = lax.all_gather(right_own, spread_axis, axis=0)
+        left_own = by_channel_share(left_fac)
+        product = jnp.einsum(
+            "cik,gcjk->gjci", left_own, right_all, preferred_element_type=jnp.float32
+        ).astype(jnp.bfloat16)
+        product = product.reshape(shares, cols, share, rows)
+        product = jnp.transpose(product, (0, 2, 3, 1))
+    merged = lax.all_to_all(
+        product.reshape(shares, share, rows * cols), share_axis, split_axis=0, concat_axis=0
+    ).reshape(width_tri, rows * cols)
     sigmoid_switches = jax.nn.sigmoid(
         jnp.einsum("ijc,cd->ijd", tri_normed, w_gate, preferred_element_type=jnp.float32)
     )
-    left_split, right_split = (
-        lax.all_to_all(left_fac, "dap", split_axis=1, concat_axis=2, tiled=True),
-        lax.all_to_all(right_fac, "dap", split_axis=1, concat_axis=2, tiled=True),
-    )
-    if not incoming:
-        product = jnp.einsum(
-            "ick,jck->icj",
-            left_split,
-            lax.all_gather(right_split, ("branch", "tile"), axis=0, tiled=True),
-            preferred_element_type=jnp.float32,
-        )
-    else:
-        product = lax.psum_scatter(
-            jnp.einsum(
-                "kci,kcj->icj", left_split, right_split, preferred_element_type=jnp.float32
-            ).astype(jnp.bfloat16),
-            ("branch", "tile"),
-            scatter_dimension=0,
-            tiled=True,
-        ).astype(jnp.float32)
-    merged = lax.all_to_all(
-        product.astype(jnp.bfloat16), "dap", split_axis=2, concat_axis=1, tiled=True
-    )
-    product_normed = standardize_features(merged, out_gain[:, None], 1).astype(jnp.bfloat16)
-    update = jnp.einsum("icj,cz->ijz", product_normed, w_out, preferred_element_type=jnp.float32)
-    return duo_hidden_values + sigmoid_switches * update
+    product_normed = standardize_features(merged, out_gain[:, None], 0).astype(jnp.bfloat16)
+    update = jnp.einsum("cp,cz->pz", product_normed, w_out, preferred_element_type=jnp.float32)
+    return duo_hidden_values + sigmoid_switches * update.reshape(rows, cols, width_tri)
 
 
 def body(
@@ -115,7 +126,16 @@
     local_bias = jnp.einsum(
         "ijc,ch->hij", pair_normed, duo_logit_projector, preferred_element_type=jnp.float32
     ).astype(jnp.bfloat16)
-    row_bias = lax.all_gather(local_bias, "dap", axis=2, tiled=True)
+    row_bias = lax.all_gather(
+        local_bias.reshape(number_of_heads, sites_each_shard * columns_per_device), "dap", axis=0
+    ).reshape(-1, number_of_heads, sites_each_shard, columns_per_device)
+    row_bias = jnp.transpose(row_bias, (1, 2, 0, 3)).reshape(number_of_heads, sites_each_shard, -1)
+    mask_grid = lax.all_gather(
+        homolog_valid_flags.astype(jnp.bfloat16), ("dap", "branch", "tile"), axis=0
+    ).reshape(lax.axis_size("dap"), -1, lines_each_shard, sites_each_shard)
+    mask_grid = jnp.transpose(mask_grid, (0, 2, 1, 3)).reshape(
+        lax.axis_size("dap") * lines_each_shard, -1
+    )
     lineup_standardized = standardize_features(homolog_hidden, homolog_heeded_rescale, 2).astype(
         jnp.bfloat16
     )
@@ -132,14 +152,15 @@
         ..., lineup_feature_extent : 3 * lineup_feature_extent
     ].astype(jnp.bfloat16)
     sigmoid_switches = jax.nn.sigmoid(mapped_contents[..., 3 * lineup_feature_extent :])
-    mask_as_float = homolog_valid_flags.astype(jnp.bfloat16)
     run_max = jnp.full((lines_each_shard, number_of_heads, sites_each_shard), -jnp.inf, jnp.float32)
     run_sum = jnp.zeros((lines_each_shard, number_of_heads, sites_each_shard), jnp.float32)
     run_acc = jnp.zeros(
         (lines_each_shard, number_of_heads, sites_each_shard, head_channels), jnp.float32
     )
     key_value_slice = lax.all_gather(key_value_pairs, ("branch", "tile"), axis=1, tiled=True)
-    mask_piece = lax.all_gather(mask_as_float, ("branch", "tile"), axis=1, tiled=True)
+    mask_piece = lax.dynamic_slice_in_dim(
+        mask_grid, lax.axis_index("dap") * lines_each_shard, lines_each_shard, axis=0
+    )
     slice_length = key_value_slice.shape[1]
     key_per_head = key_value_slice[..., :lineup_feature_extent].reshape(
         lines_each_shard, slice_length, number_of_heads, head_channels
@@ -193,41 +214,30 @@
         )
         * homolog_valid_flags.astype(jnp.float32)[..., None]
     )
-    left_flat = (
-        factors[..., :outer_channels]
-        .astype(jnp.bfloat16)
-        .reshape(lines_each_shard, sites_each_shard * outer_channels)
-    )
-    right_flat = (
-        factors[..., outer_channels:]
-        .astype(jnp.bfloat16)
-        .reshape(lines_each_shard, sites_each_shard * outer_channels)
-    )
-    right_all, mask_all = (
-        lax.all_gather(right_flat, ("branch", "tile"), axis=1, tiled=True),
-        lax.all_gather(mask_as_float, ("branch", "tile"), axis=1, tiled=True),
-    )
-    total_res = mask_all.shape[1]
-    right_all = right_all.reshape(lines_each_shard, total_res, outer_channels)
-    right_factor_rows, mask_right = (
-        lax.all_to_all(right_all, "dap", split_axis=1, concat_axis=0, tiled=True),
-        lax.all_to_all(mask_all, "dap", split_axis=1, concat_axis=0, tiled=True),
-    )
-    left_factor_rows, mask_rows = (
-        lax.all_gather(left_flat, "dap", axis=0, tiled=True),
-        lax.all_gather(mask_as_float, "dap", axis=0, tiled=True),
-    )
-    alignment_rows = left_factor_rows.shape[0]
-    left_factor_rows = left_factor_rows.reshape(alignment_rows, sites_each_shard, outer_channels)
+    factors = factors.astype(jnp.bfloat16)
+    all_factors = lax.all_gather(factors, ("dap", "branch", "tile"), axis=0).reshape(
+        lax.axis_size("dap"), -1, lines_each_shard, sites_each_shard, 2 * outer_channels
+    )
+    alignment_rows = mask_grid.shape[0]
+    left_rows = lax.dynamic_index_in_dim(
+        all_factors, lax.axis_index(("branch", "tile")), axis=1, keepdims=False
+    )[..., :outer_channels].reshape(alignment_rows, sites_each_shard, outer_channels)
+    block = col_start // sites_each_shard
+    right_rows = lax.dynamic_index_in_dim(all_factors, block, axis=1, keepdims=False)[
+        ..., outer_channels:
+    ].reshape(alignment_rows, sites_each_shard, outer_channels)
+    right_rows = lax.dynamic_slice_in_dim(
+        right_rows, col_start - block * sites_each_shard, columns_per_device, axis=1
+    )
+    mask_rows = lax.dynamic_slice_in_dim(mask_grid, row_start, sites_each_shard, axis=1)
+    mask_right = lax.dynamic_slice_in_dim(mask_grid, col_start, columns_per_device, axis=1)
     counts = jnp.einsum("si,sj->ij", mask_rows, mask_right, preferred_element_type=jnp.float32)
-    outer_prod = jnp.einsum(
-        "sic,sjd->ijcd", left_factor_rows, right_factor_rows, preferred_element_type=jnp.float32
+    exit_by_channel = dyadic_exit_projector.reshape(outer_channels, outer_channels, -1)
+    spread_right = jnp.einsum(
+        "sjd,cdz->scjz", right_rows, exit_by_channel, preferred_element_type=jnp.float32
     ).astype(jnp.bfloat16)
-    outer_prod = outer_prod.reshape(
-        sites_each_shard, columns_per_device, outer_channels * outer_channels
-    )
     update = jnp.einsum(
-        "ijk,kz->ijz", outer_prod, dyadic_exit_projector, preferred_element_type=jnp.float32
+        "sic,scjz->ijz", left_rows, spread_right, preferred_element_type=jnp.float32
     )
     duo_hidden_values = duo_hidden_values + update / (count_eps + counts)[..., None]
     for threefold_module in range(2):

time: 530 us -> 459 us (0.87)
  local copies, waits for them, and re-layouts: 169 us -> 90.2 us
  blocking collectives: 119 us -> 140 us
  starting transfers between devices: 26.7 us -> 8.6 us
  waiting for transfers between devices: 117 us -> 123 us
    all_gather x1 -> x3, waiting for transfers between devices: 0.02 us -> 88.3 us  [the longest x1 50.3 us: threeway_update(): left_all = lax.all_gather(left_own, spread_axis, axis=0)]
    convert_element_type x9 -> x5, local copies, waits for them, and re-layouts: 64.5 us -> 13.1 us  [the longest x3 6.19 us: body(): key_bias = row_bias.astype(jnp.float32)]
    unnamed x79 -> x54, local copies, waits for them, and re-layouts: 51.9 us -> 2.61 us
    reshape x6 -> x13, local copies, waits for them, and re-layouts: 1.84 us -> 47.8 us  [the longest x8 31.4 us: by_channel_share(): got = got.reshape(shares, share, kept, summed)]
    reduce_scatter x1 -> x0, waiting for transfers between devices: 44.2 us -> none  [threeway_update(): lax.psum_scatter(jnp.einsum('kci,kcj->icj', left_split, right_split, pref...]
    all_to_all x6 -> x2, waiting for transfers between devices: 73 us -> 34.6 us  [threeway_update(): lax.all_to_all(product.reshape(shares, share, rows * cols), share_axis, s...]
    all_to_all x2 -> x4, blocking collectives: 57 us -> 93.8 us  [by_channel_share(): lax.all_to_all(factor.reshape(shares, share, kept * summed), share_axis,...]
    all_to_all x11 -> x0, local copies, waits for them, and re-layouts: 33.3 us -> none  [the longest x4 16.8 us: threeway_update(): lax.all_to_all(right_fac, 'dap', split_axis=1, concat_axis=2, tiled=True)]
  transfers between devices with their start and end apart: 9 -> 6, of which waited for: 5 -> 4; matrix products, arithmetic and copies ran while one was open for 9% -> 9% of each run, Pallas kernels for 0% -> 0%
where the time goes in v1:
time: 459 us; the launch traced here: 451 us
  blocking collectives  140 us (31%)
  waiting for transfers between devices  123 us (27%)
  local copies, waits for them, and re-layouts  90.2 us (20%)
  matrix products  47.5 us (10%)
  other arithmetic  27.1 us (6%)
  between operations  14.9 us (3%)
  starting transfers between devices  8.6 us (2%)
    all_to_all x4, blocking collectives, by_channel_share(): lax.all_to_all(factor.reshape(shares, share, kept * summed), share_axis,...  93.8 us
    all_gather x1, waiting for transfers between devices, threeway_update(): left_all = lax.all_gather(left_own, spread_axis, axis=0)  50.3 us
    all_gather x1, waiting for transfers between devices, body(): lax.all_gather(factors, ('dap', 'branch', 'tile'), axis=0)  38 us
    all_to_all x2, waiting for transfers between devices, threeway_update(): lax.all_to_all(product.reshape(shares, share, rows * cols), share_axis, s...  34.6 us
    reshape x8, local copies, waits for them, and re-layouts, by_channel_share(): got = got.reshape(shares, share, kept, summed)  31.4 us
    all_gather x1, blocking collectives, body(): lax.all_gather(homolog_valid_flags.astype(jnp.bfloat16), ('dap', 'branch'...  30.2 us
    all_gather x1, blocking collectives, body(): lax.all_gather(local_bias.reshape(number_of_heads, sites_each_shard * col...  15.6 us
    dot_general x1, matrix products, body(): jnp.einsum('sic,scjz->ijz', left_rows, spread_right, preferred_element_ty...  9.77 us
  transfers between devices with their start and end apart: 6, of which 4 were waited for; matrix products, arithmetic and copies ran while one was open for 9% of the time, Pallas kernels for 0%

profile of v1, /device:TPU:0, one launch (start us, length us, event | category | flops | bytes accessed | tf_op | source)
XLA Modules:
  0.0 450.8 jit_solution(7670035700471580320)
XLA Ops:
  19.0 15.6 %all_gather.25 = bf16[4,8,4096]{2,1,0:T(8,128)(2,1)S(1)} all-gather(bf16[1,8,4096]{2,1,0:T(8,128)(2,1)S(1)} %all_gather_reshape.9), channel_id=1, replica_groups=mesh['groups'=2,'branch'=2,'dap'=4,'tile'=2] {'dap'}, dimensions={0}, use_global_device_ids=true | all-gather | bytes 327680 | tf_op jit(solution)/shard_map/all_gather | solution.py:129
  40.8 30.2 %all-gather = bf16[128,64]{1,0:T(8,128)(2,1)S(1)} all-gather(bf16[8,64]{1,0:T(8,128)(2,1)S(1)} %get-tuple-element.15), channel_id=2, replica_groups=mesh['groups'=2,'branch'=2,'dap'=4,'tile'=2] {'dap','branch','tile'}, dimensions={0}, use_global_device_ids=true | all-gather | bytes 17408 | tf_op jit(solution)/shard_map/all_gather | solution.py:133
  84.5 4.8 %fusion.53 = f32[8,64,8,32]{1,3,2,0:T(8,128)} fusion(bf16[8,256,8,32]{1,3,2,0:T(8,128)(2,1)} %bitcast.191, f32[8,8,64,256]{3,2,1,0:T(8,128)} %copy-done.6, f32[8,8,64]{2,1,0:T(8,128)S(1)} %get-tuple-element.26, f32[8,256]{1,0:T(8,128)S(1)} %add_multiply_fusion, f32[8,64,256]{2,1,0:T(8,128)S(1)} %reshape.297, f32[8,64,8]{1,2,0:T(8,128)S(1)} %bitcast_add_fusion, ...), kind=kOutput, calls=%fused_computation.82 | convolution fusion | flops 71565312 | bytes 6348800 | tf_op jit(solution)/shard_map/shij,sjhd->shid/dot_general | solution.py:184
  94.9 38.0 %all-gather.13.cloned.1.call-done = bf16[128,64,64]{2,1,0:T(8,128)(2,1)} async-done(((bf16[8,64,64]{2,1,0:T(8,128)(2,1)}), bf16[128,64,64]{2,1,0:T(8,128)(2,1)}) %all-gather.13.cloned.1.call-update) | async-done | bytes 1048592 | tf_op jit(solution)/shard_map/all_gather | solution.py:218
  134.9 9.8 %fusion.41 = f32[64,64,128]{2,0,1:T(8,128)} fusion(bf16[32,32,128,1]{2,1,0,3:T(8,128)(2,1)} %bitcast.196, bf16[4,8,64,32]{3,2,1,0:T(8,128)(2,1)S(1)} %slice.107, bf16[4,8,64,32]{2,1,0,3:T(8,128)(2,1)S(1)} %copy.120), kind=kOutput, calls=%fused_computation.72 | convolution fusion | flops 1619001344 | bytes 2621440 | tf_op jit(solution)/shard_map/sic,scjz->ijz/dot_general | solution.py:239
  144.6 3.3 fusion.117
  153.0 29.7 %all_to_all.30 = bf16[4,32,4096]{2,1,0:T(8,128)(2,1)} all-to-all(bf16[4,32,4096]{2,1,0:T(8,128)(2,1)S(1)} %bitcast.182), channel_id=1, replica_groups=mesh['groups'=2,'branch'=2,'dap'=4,'tile'=2] {'dap'}, dimensions={0} | all-to-all | bytes 2097152 | tf_op jit(solution)/shard_map/all_to_all | solution.py:48
  182.7 4.2 reshape.285
  187.0 4.9 %copy.153 = bf16[4,32,64,64]{3,0,2,1:T(4,128)(2,1)} copy(bf16[4,32,64,64]{3,2,1,0:T(8,128)(2,1)} %reshape.285) | data formatting | bytes 2097152 | tf_op jit(solution)/shard_map/reshape | solution.py:51
  191.8 4.3 all_gather_reshape.10
  196.2 28.6 %all_to_all.31 = bf16[4,32,4096]{2,1,0:T(8,128)(2,1)} all-to-all(bf16[4,32,4096]{2,1,0:T(8,128)(2,1)S(1)} %bitcast.180), channel_id=1, replica_groups=mesh['groups'=2,'branch'=2,'dap'=4,'tile'=2] {'dap'}, dimensions={0} | all-to-all | bytes 2097152 | tf_op jit(solution)/shard_map/all_to_all | solution.py:48
  224.8 4.3 reshape.287
  229.1 4.9 %copy.152 = bf16[4,32,64,64]{3,0,2,1:T(4,128)(2,1)} copy(bf16[4,32,64,64]{3,2,1,0:T(8,128)(2,1)} %reshape.287) | data formatting | bytes 2097152 | tf_op jit(solution)/shard_map/reshape | solution.py:51
  234.0 3.5 reshape.315
  237.5 4.8 %convert_bitcast_fusion.1 = bf16[4,32,64,64]{2,3,0,1:T(8,128)(2,1)} fusion(bf16[4,32,64,256]{3,2,0,1:T(8,128)(2,1)} %all-gather.9.cloned.1.call-done, bf16[32,64,256,1]{2,1,0,3:T(8,128)(2,1)S(1)} %reshape.315), kind=kOutput, calls=%fused_computation.61 | convolution fusion | flops 268959744 | bytes 6291456 | tf_op jit(solution)/shard_map/cik,gcjk->gjci/dot_general | solution.py:67
  242.3 4.1 copy.125
  246.4 4.2 reshape.289
  250.6 3.5 all-to-all-start.2
  256.3 22.6 %all-to-all-done.2 = bf16[4,32,4096]{2,1,0:T(8,128)(2,1)S(1)} async-done(((bf16[4,32,4096]{2,1,0:T(8,128)(2,1)}), bf16[4,32,4096]{2,1,0:T(8,128)(2,1)S(1)}, u32[]{:S(2)}, u32[]{:S(2)}) %all-to-all-start.2) | async-done | bytes 1048608 | tf_op jit(solution)/shard_map/all_to_all | solution.py:72
  294.2 17.6 %all_to_all.32 = bf16[4,32,4096]{2,1,0:T(8,128)(2,1)} all-to-all(bf16[4,32,4096]{2,1,0:T(8,128)(2,1)S(1)} %bitcast.183), channel_id=1, replica_groups=mesh['groups'=2,'branch'=2,'dap'=4,'tile'=2] {'branch','tile'}, dimensions={0} | all-to-all | bytes 2097152 | tf_op jit(solution)/shard_map/all_to_all | solution.py:48
  315.1 3.3 copy.150
  318.4 4.4 all_gather_reshape.11
  322.9 17.8 %all_to_all.33 = bf16[4,32,4096]{2,1,0:T(8,128)(2,1)} all-to-all(bf16[4,32,4096]{2,1,0:T(8,128)(2,1)S(1)} %bitcast.181), channel_id=1, replica_groups=mesh['groups'=2,'branch'=2,'dap'=4,'tile'=2] {'branch','tile'}, dimensions={0} | all-to-all | bytes 2097152 | tf_op jit(solution)/shard_map/all_to_all | solution.py:48
  340.7 3.3 reshape.292
  344.0 3.3 copy.151
  347.3 4.3 reshape.318
  351.6 50.3 %all-gather.11.cloned.1.call-done = bf16[4,32,64,256]{3,2,0,1:T(8,128)(2,1)} async-done(((bf16[1,32,64,256]{3,2,0,1:T(8,128)(2,1)}), bf16[4,32,64,256]{3,2,0,1:T(8,128)(2,1)}) %all-gather.11.cloned.1.call-update) | async-done | bytes 4194320 | tf_op jit(solution)/shard_map/all_gather | solution.py:56
  401.9 4.6 %convert_bitcast_fusion = bf16[4,32,64,64]{2,3,0,1:T(8,128)(2,1)S(1)} fusion(bf16[4,32,64,256]{3,2,0,1:T(8,128)(2,1)} %all-gather.11.cloned.1.call-done, bf16[32,64,256,1]{2,1,0,3:T(8,128)(2,1)} %reshape.318), kind=kOutput, calls=%fused_computation.56 | convolution fusion | flops 268959744 | bytes 6291456 | tf_op jit(solution)/shard_map/gcik,cjk->gicj/dot_general | solution.py:58
  409.4 4.3 reshape.296
  413.7 4.2 all-to-all-start.5
  420.5 12.0 %all-to-all-done.5 = bf16[4,32,4096]{2,1,0:T(8,128)(2,1)} async-done(((bf16[4,32,4096]{2,1,0:T(8,128)(2,1)}), bf16[4,32,4096]{2,1,0:T(8,128)(2,1)}, u32[]{:S(2)}, u32[]{:S(2)}) %all-to-all-start.5) | async-done | bytes 1048608 | tf_op jit(solution)/shard_map/all_to_all | solution.py:72
  440.2 3.6 add_convert_fusion
  (141 shorter events, 77.6 us)
Async XLA Ops:
  7.2 2.5 copy-start
  7.2 65.3 %all-gather.7.cloned.1.call-start = ((), (), s32[]{:S(2)}) async-start(), calls=%async_computation.6 | async-start | bytes 2621440 | tf_op jit(solution)/shard_map/all_gather | solution.py:160
  9.6 3.8 copy-start.18
  9.6 3.8 copy-start.19
  9.6 3.9 copy-start.15
  11.1 1.3 copy-start.8
  13.3 119.6 %all-gather.13.cloned.1.call-start = ((), (), s32[]{:S(2)}) async-start(), calls=%async_computation.9 | async-start | bytes 2228224 | tf_op jit(solution)/shard_map/all_gather | solution.py:218
  13.6 3.7 copy-start.17
  13.6 3.7 copy-start.22
  36.0 4.7 %copy-start.16 = (s32[8,64]{1,0:T(8,128)S(1)}, s32[8,64]{1,0:T(8,128)}, u32[]{:S(2)}) copy-start(s32[8,64]{1,0:T(8,128)} %param.22) | copy-start | bytes 6148
  80.2 1.9 copy-start.6
  84.5 6.3 %copy-start.10 = (bf16[8,64,256]{2,1,0:T(8,128)(2,1)S(1)}, bf16[8,64,256]{2,1,0:T(8,128)(2,1)}, u32[]{:S(2)}) copy-start(bf16[8,64,256]{2,1,0:T(8,128)(2,1)} %param.20) | copy-start | bytes 786436
  84.5 6.4 %copy-start.23 = (bf16[256,256]{1,0:T(8,128)(2,1)S(1)}, bf16[256,256]{1,0:T(8,128)(2,1)}, u32[]{:S(2)}) copy-start(bf16[256,256]{1,0:T(8,128)(2,1)} %param.31) | copy-start | bytes 393220
  89.3 3.7 copy-start.25
  89.3 3.7 copy-start.26
  90.8 3.7 copy-start.14
  90.9 4.0 copy-start.20
  94.0 143.5 %all-gather.9.cloned.1.call-start = ((), (), s32[]{:S(2)}) async-start(), calls=%async_computation.7 | async-start | bytes 5242880 | tf_op jit(solution)/shard_map/all_gather | solution.py:65
  147.9 2.7 copy-start.2
  149.3 1.3 copy-start.11
  246.4 8.1 %copy-start.21 = (f32[2,128]{1,0:T(2,128)S(1)}, f32[2,128]{1,0:T(2,128)}, u32[]{:S(2)}) copy-start(f32[2,128]{1,0:T(2,128)} %param.38) | copy-start | bytes 3076
  246.4 8.1 %copy-start.13 = (bf16[2,128,128]{2,1,0:T(8,128)(2,1)S(1)}, bf16[2,128,128]{2,1,0:T(8,128)(2,1)}, u32[]{:S(2)}) copy-start(bf16[2,128,128]{2,1,0:T(8,128)(2,1)} %param.37) | copy-start | bytes 196612
  250.6 28.3 %all-to-all-start.2 = ((bf16[4,32,4096]{2,1,0:T(8,128)(2,1)}), bf16[4,32,4096]{2,1,0:T(8,128)(2,1)S(1)}, u32[]{:S(2)}, u32[]{:S(2)}) async-start(bf16[4,32,4096]{2,1,0:T(8,128)(2,1)} %reshape.289), calls=%async_computation.2 | async-start | bytes 2097152 | tf_op jit(solution)/shard_map/all_to_all | solution.py:72
  254.1 147.8 %all-gather.11.cloned.1.call-start = ((), (), s32[]{:S(2)}) async-start(), calls=%async_computation.8 | async-start | bytes 5242880 | tf_op jit(solution)/shard_map/all_gather | solution.py:56
  278.8 1.0 copy-start.7
  279.8 4.9 %copy-start.3 = (f32[64,64,128]{2,1,0:T(8,128)S(1)}, f32[64,64,128]{2,1,0:T(8,128)}, u32[]{:S(2)}) copy-start(f32[64,64,128]{2,1,0:T(8,128)} %copy-done.2) | copy-start | bytes 6291460
  279.8 4.9 %copy-start.24 = (bf16[2,128,128]{2,1,0:T(8,128)(2,1)S(1)}, bf16[2,128,128]{2,1,0:T(8,128)(2,1)}, u32[]{:S(2)}) copy-start(bf16[2,128,128]{2,1,0:T(8,128)(2,1)} %param.39) | copy-start | bytes 196612
  287.5 2.6 copy-start.4
  318.4 4.5 copy-start.9
  409.4 8.6 %copy-start.5 = (f32[64,64,128]{2,1,0:T(8,128)S(1)}, f32[64,64,128]{2,1,0:T(8,128)}, u32[]{:S(2)}) copy-start(f32[64,64,128]{2,1,0:T(8,128)} %copy-done.4) | copy-start | bytes 6291460
  413.7 18.8 %all-to-all-start.5 = ((bf16[4,32,4096]{2,1,0:T(8,128)(2,1)}), bf16[4,32,4096]{2,1,0:T(8,128)(2,1)}, u32[]{:S(2)}, u32[]{:S(2)}) async-start(bf16[4,32,4096]{2,1,0:T(8,128)(2,1)} %reshape.296), calls=%async_computation.5 | async-start | bytes 2097152 | tf_op jit(solution)/shard_map/all_to_all | solution.py:72
  440.2 3.6 copy-start.1
  (1 other events, 0.7 us)
Sparse Core Ops, SparseCore 0:
  13.4 25.2 all-gather.6
  94.1 38.7 all-gather.12
  196.3 32.5 all-gather.8
  323.0 78.8 all-gather.10

commit v2 on v1

--- a/solution.py
+++ b/solution.py
@@ -1,6 +1,10 @@
+import functools
+
 import jax
 import jax.numpy as jnp
 from jax import lax
+from jax.experimental import pallas as pl
+from jax.experimental.pallas import tpu as pltpu
 from jax.sharding import PartitionSpec as P
 
 REL_BINS = 66
@@ -78,6 +82,343 @@
     product_normed = standardize_features(merged, out_gain[:, None], 0).astype(jnp.bfloat16)
     update = jnp.einsum("cp,cz->pz", product_normed, w_out, preferred_element_type=jnp.float32)
     return duo_hidden_values + sigmoid_switches * update.reshape(rows, cols, width_tri)
+
+
+MESH = pl.DeviceIdType.MESH
+LANES = 128
+
+
+def start_remote(src, dst, send_sem, recv_sem, device):
+    copy = pltpu.make_async_remote_copy(
+        src_ref=src,
+        dst_ref=dst,
+        send_sem=send_sem,
+        recv_sem=recv_sem,
+        device_id=device,
+        device_id_type=MESH,
+    )
+    copy.start()
+    return copy
+
+
+def triangle_kernel(
+    incoming,
+    own_in,
+    spread_in,
+    state,
+    normed,
+    w_gate,
+    out_gain,
+    w_out,
+    out,
+    own,
+    spread,
+    own_wide,
+    spread_wide,
+    product_wide,
+    outgoing_blocks,
+    merged,
+    trade_send,
+    trade_recv,
+    local_sem,
+    spread_send,
+    spread_recv,
+    back_send,
+    back_recv,
+):
+    n, pairs, share = own.shape[0], own.shape[1], own.shape[2]
+    m = spread.shape[0]
+    half = LANES // 2
+    tiles = lax.axis_size("tile")
+    branch, tile, dap = lax.axis_index("branch"), lax.axis_index("tile"), lax.axis_index("dap")
+    block = branch * tiles + tile
+
+    def by_block(index):
+        return {"branch": index // tiles, "tile": lax.rem(index, tiles)}
+
+    def by_dap(index):
+        return {"dap": index}
+
+    if incoming:
+        me, trade_to, place, spread_to = block, by_block, dap, by_dap
+    else:
+        me, trade_to, place, spread_to = dap, by_dap, block, by_block
+
+    barrier = pltpu.get_barrier_semaphore()
+    for k in range(1, n):
+        pl.semaphore_signal(
+            barrier, inc=1, device_id=trade_to(lax.rem(me + k, n)), device_id_type=MESH
+        )
+    for k in range(1, m):
+        pl.semaphore_signal(
+            barrier, inc=1, device_id=spread_to(lax.rem(place + k, m)), device_id_type=MESH
+        )
+    pl.semaphore_wait(barrier, n + m - 2)
+
+    def channels(ref, index):
+        return ref.at[:, pl.ds(pl.multiple_of(index * share, share), share), :]
+
+    trades = [[], []]
+    for which, (src, dst) in enumerate(((spread_in, spread.at[place, me]), (own_in, own.at[me]))):
+        for k in range(1, n):
+            to = lax.rem(me + k, n)
+            trades[which].append(
+                start_remote(
+                    channels(src, to),
+                    dst,
+                    trade_send.at[which, k - 1],
+                    trade_recv.at[which, k - 1],
+                    trade_to(to),
+                )
+            )
+    locals_ = [
+        pltpu.make_async_copy(channels(spread_in, me), spread.at[place, me], local_sem.at[0]),
+        pltpu.make_async_copy(channels(own_in, me), own.at[me], local_sem.at[1]),
+    ]
+    for copy in locals_:
+        copy.start()
+
+    def widen(dst, load):
+        def step(s, _):
+            dst[pl.ds(pl.multiple_of(s * pairs * share, share), pairs * share), :] = (
+                load(s).astype(jnp.float32).reshape(pairs * share, LANES)
+            )
+            return 0
+
+        lax.fori_loop(0, n, step, 0)
+
+    def matrix(ref, c):
+        lower = lax.broadcasted_iota(jnp.int32, (pairs, LANES), 1) < half
+        columns = []
+        for s in range(0, n, 2):
+            first = ref[pl.ds(s * pairs * share + c, pairs, stride=share), :]
+            second = ref[pl.ds((s + 1) * pairs * share + c, pairs, stride=share), :]
+            top = jnp.where(lower, first, pltpu.roll(second, half, 1))
+            bottom = jnp.where(lower, pltpu.roll(first, half, 1), second)
+            columns.append(jnp.concatenate([top, bottom], axis=0))
+        return jnp.concatenate(columns, axis=1).astype(jnp.bfloat16)
+
+    def multiply(g):
+        widen(spread_wide, lambda s: spread[g, s])
+
+        def step(c, _):
+            mine, other = matrix(own_wide, c), matrix(spread_wide, c)
+            left, right = (other, mine) if incoming else (mine, other)
+            found = lax.dot_general(
+                left, right, (((1,), (1,)), ((), ())), preferred_element_type=jnp.float32
+            )
+            product_wide[pl.ds(c, pairs, stride=share), :] = jnp.concatenate(
+                [found[:pairs], found[pairs:]], axis=1
+            )
+            return 0
+
+        lax.fori_loop(0, share, step, 0, unroll=4)
+        outgoing_blocks[g] = (
+            product_wide[...].reshape(pairs, share, LANES).astype(jnp.bfloat16)
+        )
+
+        @pl.when(g != me)
+        def _():
+            start_remote(
+                outgoing_blocks.at[g],
+                merged.at[me],
+                back_send.at[g],
+                back_recv.at[me],
+                trade_to(g),
+            )
+
+        @pl.when(g == me)
+        def _():
+            merged[g] = outgoing_blocks[g]
+
+    def spread_copy(g, k, slot, device):
+        piece = spread.at[g, lax.rem(me - k + n, n)]
+        return pltpu.make_async_remote_copy(
+            src_ref=piece,
+            dst_ref=piece,
+            send_sem=spread_send.at[slot, k],
+            recv_sem=spread_recv.at[slot, k],
+            device_id=device,
+            device_id_type=MESH,
+        )
+
+    def finish_own():
+        locals_[1].wait()
+        for copy in trades[1]:
+            copy.wait()
+        widen(own_wide, lambda s: own[s])
+
+    if incoming:
+        right, left = place + 1, place - 1
+        has_right, has_left = right < m, left >= 0
+        sides = ((0, 1, right, has_right), (1, -1, left, has_left))
+        for k in range(n):
+            if k == 0:
+                locals_[0].wait()
+            else:
+                trades[0][k - 1].wait()
+            for side, _, to, there in sides:
+
+                @pl.when(there)
+                def _(side=side, to=to, k=k):
+                    spread_copy(place, k, side * (m - 1), spread_to(to)).start()
+
+        finish_own()
+        multiply(place)
+        for h in range(1, m):
+            for side, sign, to, there in sides:
+                g = place - sign * h
+                has_block = (g >= 0) if sign > 0 else (g < m)
+
+                @pl.when(has_block)
+                def _(side=side, to=to, there=there, g=g, h=h):
+                    for k in range(n):
+                        spread_copy(
+                            g, k, side * (m - 1) + h - 1, spread_to(lax.rem(place + 1, m))
+                        ).wait_recv()
+                        if h < m - 1:
+
+                            @pl.when(there)
+                            def _(k=k):
+                                spread_copy(g, k, side * (m - 1) + h, spread_to(to)).start()
+
+            for side, sign, to, there in sides:
+                g = place - sign * h
+                has_block = (g >= 0) if sign > 0 else (g < m)
+
+                @pl.when(has_block)
+                def _(g=g):
+                    multiply(g)
+
+        for side, sign, to, there in sides:
+            for h in range(m - 1):
+                g = place - sign * h
+                has_block = (g >= 0) if sign > 0 else (g < m)
+
+                @pl.when(jnp.logical_and(there, has_block))
+                def _(side=side, g=g, h=h, to=to):
+                    for k in range(n):
+                        spread_copy(g, k, side * (m - 1) + h, spread_to(to)).wait_send()
+
+    else:
+        across = (1 - branch) * tiles + tile
+        beside = branch * tiles + (1 - tile)
+        beyond = (1 - branch) * tiles + (1 - tile)
+        to_tile, to_branch = spread_to(beside), spread_to(across)
+        copies = []
+        for k in range(n):
+            if k == 0:
+                locals_[0].wait()
+            else:
+                trades[0][k - 1].wait()
+            for slot, device in ((0, to_tile), (1, to_branch)):
+                copy = spread_copy(place, k, slot, device)
+                copy.start()
+                copies.append(copy)
+        finish_own()
+        for k in range(n):
+            spread_copy(beside, k, 0, to_tile).wait_recv()
+            copy = spread_copy(beside, k, 2, to_branch)
+            copy.start()
+            copies.append(copy)
+        multiply(place)
+        multiply(beside)
+        for k in range(n):
+            spread_copy(across, k, 1, to_branch).wait_recv()
+        multiply(across)
+        for k in range(n):
+            spread_copy(beyond, k, 2, to_branch).wait_recv()
+        multiply(beyond)
+        for copy in copies:
+            copy.wait_send()
+
+    for k in range(1, n):
+        source = lax.rem(me - k + n, n)
+        pltpu.make_async_remote_copy(
+            src_ref=outgoing_blocks.at[source],
+            dst_ref=merged.at[source],
+            send_sem=back_send.at[source],
+            recv_sem=back_recv.at[source],
+            device_id=trade_to(source),
+            device_id_type=MESH,
+        ).wait()
+
+    def finish(t, _):
+        found = merged[:, pl.ds(t, 1)].astype(jnp.float32).reshape(n * share, LANES)
+        centred = found - jnp.mean(found, axis=0, keepdims=True)
+        spread_of = jnp.mean(centred * centred, axis=0, keepdims=True)
+        scaled = (centred * lax.rsqrt(spread_of + norm_eps) * out_gain[...]).astype(jnp.bfloat16)
+        update = lax.dot_general(
+            scaled, w_out[...], (((0,), (0,)), ((), ())), preferred_element_type=jnp.float32
+        )
+        for part in range(2):
+            i = part * pairs + t
+            gate = jax.nn.sigmoid(
+                jnp.dot(normed[i], w_gate[...], preferred_element_type=jnp.float32)
+            )
+            out[i] = (state[i] + gate * update[part * half : (part + 1) * half]).astype(out.dtype)
+        return 0
+
+    lax.fori_loop(0, pairs, finish, 0, unroll=2)
+
+
+def fused_update(
+    state, flags, norm_gain, w_in, w_gate, out_gain, w_out, incoming, out_type
+):
+    width = w_in.shape[1] // 4
+    rows, cols = flags.shape
+    n = lax.axis_size("dap")
+    share, pairs, half = width // n, rows // 2, rows
+    normed = standardize_features(state, norm_gain, 2).astype(jnp.bfloat16)
+    flags = flags.astype(jnp.float32)
+    positions = jnp.transpose(normed, (1, 0, 2)) if incoming else normed
+    flags = flags.T if incoming else flags
+    positions = positions.reshape(2, pairs, half, width).transpose(1, 0, 2, 3)
+    flags = flags.reshape(2, pairs, half).transpose(1, 0, 2).reshape(pairs, 1, LANES)
+    mapped = jnp.einsum(
+        "tpc,cd->tdp",
+        positions.reshape(pairs, LANES, width),
+        w_in,
+        preferred_element_type=jnp.float32,
+    )
+    blocks = [mapped[:, q * width : (q + 1) * width] for q in range(4)]
+    left = (jax.nn.sigmoid(blocks[1]) * blocks[0] * flags).astype(jnp.bfloat16)
+    right = (jax.nn.sigmoid(blocks[3]) * blocks[2] * flags).astype(jnp.bfloat16)
+    own, spread = (right, left) if incoming else (left, right)
+    slots = 2 * (n - 1)
+    vmem = pl.BlockSpec(memory_space=pltpu.VMEM)
+    factor = (n, pairs, share, LANES)
+    return pl.pallas_call(
+        functools.partial(triangle_kernel, incoming),
+        out_shape=jax.ShapeDtypeStruct(state.shape, out_type),
+        in_specs=[vmem] * 7,
+        out_specs=vmem,
+        scratch_shapes=[
+            pltpu.VMEM(factor, jnp.bfloat16),
+            pltpu.VMEM((n, *factor), jnp.bfloat16),
+            pltpu.VMEM((n * pairs * share, LANES), jnp.float32),
+            pltpu.VMEM((n * pairs * share, LANES), jnp.float32),
+            pltpu.VMEM((pairs * share, LANES), jnp.float32),
+            pltpu.VMEM(factor, jnp.bfloat16),
+            pltpu.VMEM(factor, jnp.bfloat16),
+            pltpu.SemaphoreType.DMA((2, n - 1)),
+            pltpu.SemaphoreType.DMA((2, n - 1)),
+            pltpu.SemaphoreType.DMA((2,)),
+            pltpu.SemaphoreType.DMA((slots, n)),
+            pltpu.SemaphoreType.DMA((slots, n)),
+            pltpu.SemaphoreType.DMA((n,)),
+            pltpu.SemaphoreType.DMA((n,)),
+        ],
+        compiler_params=pltpu.CompilerParams(
+            collective_id=1 if incoming else 0,
+            has_side_effects=True,
+            vmem_limit_bytes=40 * 1024 * 1024,
+        ),
+        cost_estimate=pl.CostEstimate(
+            flops=2 * 256 * rows * cols * width, bytes_accessed=8 << 20, transcendentals=0
+        ),
+        name="triangle_in" if incoming else "triangle_out",
+    )(own, spread, state, normed, w_gate, out_gain.reshape(width, 1), w_out)
 
 
 def body(
@@ -240,10 +581,13 @@
         "sic,scjz->ijz", left_rows, spread_right, preferred_element_type=jnp.float32
     )
     duo_hidden_values = duo_hidden_values + update / (count_eps + counts)[..., None]
+    square = (
+        duo_hidden.shape[:2] == (LANES // 2, LANES // 2)
+        and lax.axis_size("branch") == lax.axis_size("tile") == 2
+        and lax.axis_size("dap") == 4
+    )
     for threefold_module in range(2):
-        duo_hidden_values = threeway_update(
-            duo_hidden_values,
-            duo_valid_flags,
+        parameters = (
             triad_entry_rescales[threefold_module],
             triad_entry_projectors[threefold_module],
             triad_valve_projectors[threefold_module],
@@ -251,6 +595,13 @@
             triad_exit_projectors[threefold_module],
             threefold_module == 1,
         )
+        if square:
+            out_type = jnp.bfloat16 if threefold_module == 1 else jnp.float32
+            duo_hidden_values = fused_update(
+                duo_hidden_values, duo_valid_flags, *parameters, out_type
+            )
+        else:
+            duo_hidden_values = threeway_update(duo_hidden_values, duo_valid_flags, *parameters)
     return (lineup_updated_state, duo_hidden_values.astype(jnp.bfloat16))
 
 

time: 459 us -> 345 us (0.75); the launches traced: 451 us -> 344 us
  Pallas kernels: 0 us -> 175 us
  blocking collectives: 140 us -> 45.7 us
  waiting for transfers between devices: 123 us -> 35.8 us
  local copies, waits for them, and re-layouts: 90.2 us -> 26.9 us
  matrix products: 47.5 us -> 27.9 us
  starting transfers between devices: 8.6 us -> 0.08 us
  other arithmetic: 27.1 us -> 18.8 us
    pallas_call x0 -> x2, Pallas kernels: none -> 175 us  [fused_update(): pl.pallas_call(functools.partial(triangle_kernel, incoming), out_shape=ja...]
    all_to_all x4 -> x0, blocking collectives: 93.8 us -> none  [by_channel_share(): lax.all_to_all(factor.reshape(shares, share, kept * summed), share_axis,...]
    all_gather x2 -> x0, waiting for transfers between devices: 50.3 us -> none  [the longest x1 50.3 us: threeway_update(): left_all = lax.all_gather(left_own, spread_axis, axis=0)]
    reshape x12 -> x0, local copies, waits for them, and re-layouts: 47.7 us -> none  [the longest x8 31.4 us: by_channel_share(): got = got.reshape(shares, share, kept, summed)]
    all_to_all x2 -> x0, waiting for transfers between devices: 34.6 us -> none  [threeway_update(): lax.all_to_all(product.reshape(shares, share, rows * cols), share_axis, s...]
    dot_general x8 -> x2, matrix products: 22.6 us -> 2.58 us  [fused_update(): jnp.einsum('tpc,cd->tdp', positions.reshape(pairs, LANES, width), w_in, p...]
    another operation x2 -> x3, local copies, waits for them, and re-layouts: 8.77 us -> 0.98 us  [fused_update(): out_gain.reshape(width, 1)]
    all_to_all x2 -> x0, starting transfers between devices: 7.76 us -> none  [threeway_update(): lax.all_to_all(product.reshape(shares, share, rows * cols), share_axis, s...]
  transfers between devices with their start and end apart: 6 -> 2, of which waited for: 4 -> 1; matrix products, arithmetic and copies ran while one was open for 9% -> 5% of each run, Pallas kernels for 0% -> 0%
where the time goes in v2:
time: 345 us; the launch traced here: 344 us
  Pallas kernels  175 us (51%)
  blocking collectives  45.7 us (13%)
  waiting for transfers between devices  35.8 us (10%)
  matrix products  27.9 us (8%)
  local copies, waits for them, and re-layouts  26.9 us (8%)
  other arithmetic  18.8 us (5%)
  between operations  14.6 us (4%)
    pallas_call x2, Pallas kernels, fused_update(): pl.pallas_call(functools.partial(triangle_kernel, incoming), out_shape=ja...  175 us
    all_gather x1, waiting for transfers between devices, body(): lax.all_gather(factors, ('dap', 'branch', 'tile'), axis=0)  35.8 us
    all_gather x1, blocking collectives, body(): lax.all_gather(homolog_valid_flags.astype(jnp.bfloat16), ('dap', 'branch'...  30.1 us
    all_gather x1, blocking collectives, body(): lax.all_gather(local_bias.reshape(number_of_heads, sites_each_shard * col...  15.6 us
    dot_general x1, matrix products, body(): jnp.einsum('sic,scjz->ijz', left_rows, spread_right, preferred_element_ty...  9.95 us
  transfers between devices with their start and end apart: 2, of which 1 were waited for; matrix products, arithmetic and copies ran while one was open for 5% of the time, Pallas kernels for 0%

profile of v2, /device:TPU:0, one launch (start us, length us, event | category | flops | bytes accessed | tf_op | source)
XLA Modules:
  0.0 344.2 jit_solution(17079830520680053042)
XLA Ops:
  8.4 1.2 fusion.58
  9.7 1.4 fusion.71
  12.7 2.3 fusion.104
  15.1 1.3 multiply_reduce_fusion.2
  16.5 1.5 fusion.46
  18.1 15.6 %all_gather.19 = bf16[4,8,4096]{2,1,0:T(8,128)(2,1)S(1)} all-gather(bf16[1,8,4096]{2,1,0:T(8,128)(2,1)S(1)} %all_gather_reshape.3), channel_id=1, replica_groups=mesh['groups'=2,'branch'=2,'dap'=4,'tile'=2] {'dap'}, dimensions={0}, use_global_device_ids=true | all-gather | bytes 327680 | tf_op jit(solution)/shard_map/all_gather | solution.py:470
  33.7 1.5 reshape.220
  35.2 2.9 copy.114
  38.1 1.8 reshape.219
  40.5 30.1 %all-gather = bf16[128,64]{1,0:T(8,128)(2,1)S(1)} all-gather(bf16[8,64]{1,0:T(8,128)(2,1)S(1)} %get-tuple-element.19), channel_id=2, replica_groups=mesh['groups'=2,'branch'=2,'dap'=4,'tile'=2] {'dap','branch','tile'}, dimensions={0}, use_global_device_ids=true | all-gather | bytes 17408 | tf_op jit(solution)/shard_map/all_gather | solution.py:474
  72.9 3.1 fusion.100
  75.9 2.3 copy.112
  78.2 2.6 fusion.5
  80.8 1.6 fusion.6
  82.7 2.3 copy.116
  85.0 4.8 %fusion.47 = f32[8,64,8,32]{1,3,2,0:T(8,128)} fusion(bf16[8,256,8,32]{1,3,2,0:T(8,128)(2,1)} %bitcast.132, f32[8,8,64,256]{3,2,1,0:T(8,128)} %copy-done.1, f32[8,8,64]{2,1,0:T(8,128)S(1)} %get-tuple-element.30, f32[8,256]{1,0:T(8,128)S(1)} %add_multiply_fusion, f32[8,64,256]{2,1,0:T(8,128)S(1)} %reshape.219, f32[8,64,8]{1,2,0:T(8,128)S(1)} %bitcast_add_fusion, ...), kind=kOutput, calls=%fused_computation.64 | convolution fusion | flops 71565312 | bytes 6348800 | tf_op jit(solution)/shard_map/shij,sjhd->shid/dot_general | solution.py:525
  89.8 1.6 copy.117
  91.4 1.5 convert_reduce_fusion.1
  97.8 35.8 %all-gather.7.cloned.1.call-done = bf16[128,64,64]{2,1,0:T(8,128)(2,1)} async-done(((bf16[8,64,64]{2,1,0:T(8,128)(2,1)}), bf16[128,64,64]{2,1,0:T(8,128)(2,1)}) %all-gather.7.cloned.1.call-update) | async-done | bytes 1048592 | tf_op jit(solution)/shard_map/all_gather | solution.py:559
  133.6 1.3 dynamic-slice_bitcast_fusion.1
  137.0 9.9 %fusion.35 = f32[64,64,128]{2,0,1:T(8,128)} fusion(bf16[32,32,128,1]{2,1,0,3:T(8,128)(2,1)} %bitcast.137, bf16[4,8,64,32]{3,2,1,0:T(8,128)(2,1)} %slice.107, bf16[4,8,64,32]{2,1,0,3:T(8,128)(2,1)} %copy.118), kind=kOutput, calls=%fused_computation.54 | convolution fusion | flops 1619001344 | bytes 2621440 | tf_op jit(solution)/shard_map/sic,scjz->ijz/dot_general | solution.py:580
  147.0 3.3 fusion.98
  150.3 1.3 multiply_reduce_fusion.1
  151.6 1.2 multiply_convert_fusion.1.normed
  153.0 1.3 convolution_bitcast_fusion.1
  154.3 1.2 fusion.21
  155.4 73.4 %triangle_out.1.state = f32[64,64,128]{2,1,0:T(8,128)S(1)} custom-call(bf16[32,128,128]{2,1,0:T(8,128)(2,1)S(1)} %get-tuple-element.7.own_in, bf16[32,128,128]{2,1,0:T(8,128)(2,1)S(1)} %get-tuple-element.6.spread_in, f32[64,64,128]{2,1,0:T(8,128)S(1)} %get-tuple-element.3.state, bf16[64,64,128]{2,1,0:T(8,128)(2,1)S(1)} %multiply_convert_fusion.1.normed, ...), custom_call_target="tpu_custom_call" | custom-call | flops 268435456 | bytes 8388608 | tf_op jit(solution)/shard_map/triangle_out/pallas_call | solution.py:391
  229.5 1.3 multiply_reduce_fusion
  230.8 1.2 multiply_convert_fusion.normed
  232.8 1.3 convolution_bitcast_fusion
  234.1 1.2 fusion.11
  235.3 101.2 %triangle_in.1 = bf16[64,64,128]{2,1,0:T(8,128)(2,1)S(1)} custom-call(bf16[32,128,128]{2,1,0:T(8,128)(2,1)S(1)} %get-tuple-element.5.own_in, bf16[32,128,128]{2,1,0:T(8,128)(2,1)S(1)} %get-tuple-element.4.spread_in, f32[64,64,128]{2,1,0:T(8,128)S(1)} %triangle_out.1.state, bf16[64,64,128]{2,1,0:T(8,128)(2,1)S(1)} %multiply_convert_fusion.normed, ...), custom_call_target="tpu_custom_call" | custom-call | flops 268435456 | bytes 8388608 | tf_op jit(solution)/shard_map/triangle_in/pallas_call | solution.py:391
  (83 shorter events, 15.5 us)
Async XLA Ops:
  7.2 2.5 copy-start
  7.2 65.7 %all-gather.5.cloned.1.call-start = ((), (), s32[]{:S(2)}) async-start(), calls=%async_computation | async-start | bytes 2621440 | tf_op jit(solution)/shard_map/all_gather | solution.py:501
  9.6 2.6 copy-start.12
  9.6 2.5 copy-start.13
  9.6 3.1 copy-start.8
  11.1 1.5 copy-start.2
  12.1 121.5 %all-gather.7.cloned.1.call-start = ((), (), s32[]{:S(2)}) async-start(), calls=%async_computation.1 | async-start | bytes 2228224 | tf_op jit(solution)/shard_map/all_gather | solution.py:559
  12.7 3.7 %copy-start.11 = (bf16[128,8]{0,1:T(8,128)(2,1)S(1)}, bf16[128,8]{0,1:T(8,128)(2,1)}, u32[]{:S(2)}) copy-start(bf16[128,8]{0,1:T(8,128)(2,1)} %param.28) | copy-start | bytes 6148
  12.7 3.7 %copy-start.14 = (f32[128]{0:T(128)S(1)}, f32[128]{0:T(128)}, u32[]{:S(2)}) copy-start(f32[128]{0:T(128)} %param.27) | copy-start | bytes 1540
  35.2 4.8 %copy-start.9 = (s32[8,64]{1,0:T(8,128)S(1)}, s32[8,64]{1,0:T(8,128)}, u32[]{:S(2)}) copy-start(s32[8,64]{1,0:T(8,128)} %param.22) | copy-start | bytes 6148
  80.8 1.9 copy-start.1
  85.0 6.4 %copy-start.3 = (bf16[8,64,256]{2,1,0:T(8,128)(2,1)S(1)}, bf16[8,64,256]{2,1,0:T(8,128)(2,1)}, u32[]{:S(2)}) copy-start(bf16[8,64,256]{2,1,0:T(8,128)(2,1)} %param.20) | copy-start | bytes 786436
  89.8 3.8 %copy-start.10 = (f32[8,64]{1,0:T(8,128)S(1)}, f32[8,64]{1,0:T(8,128)}, u32[]{:S(2)}) copy-start(f32[8,64]{1,0:T(8,128)} %get-tuple-element.18) | copy-start | bytes 6148
  89.8 3.8 %copy-start.16 = (f32[256]{0:T(256)S(1)}, f32[256]{0:T(256)}, u32[]{:S(2)}) copy-start(f32[256]{0:T(256)} %param.32) | copy-start | bytes 3076
  91.4 2.2 copy-start.15
  91.4 3.2 copy-start.7
  91.4 5.6 %copy-start.6 = (bf16[2,128,128]{2,1,0:T(8,128)(2,1)S(1)}, bf16[2,128,128]{2,1,0:T(8,128)(2,1)}, u32[]{:S(2)}) copy-start(bf16[2,128,128]{2,1,0:T(8,128)(2,1)} %param.39) | copy-start | bytes 196612
  92.9 0.7 copy-start.5
  151.6 1.4 copy-start.4
Sparse Core Ops, SparseCore 0:
  12.2 25.2 all-gather.4
  94.7 38.7 all-gather.6

commit v3 on v2

--- a/solution.py
+++ b/solution.py
@@ -421,6 +421,256 @@
     )(own, spread, state, normed, w_gate, out_gain.reshape(width, 1), w_out)
 
 
+def attention_kernel(
+    heads, query, own_kv, own_bias, own_mask, out, kv, bias, mask, bias_wide, mask_wide,
+    kv_send, kv_recv, bias_send, bias_recv, mask_send, mask_recv,
+):
+    tiles = lax.axis_size("tile")
+    n, m = bias.shape[0], kv.shape[0]
+    lines, sites, width = query.shape
+    half = LANES // 2
+    branch, tile, dap = lax.axis_index("branch"), lax.axis_index("tile"), lax.axis_index("dap")
+    place = branch * tiles + tile
+
+    def at(index):
+        return {"branch": index // tiles, "tile": lax.rem(index, tiles)}
+
+    barrier = pltpu.get_barrier_semaphore()
+    for k in range(1, n):
+        pl.semaphore_signal(
+            barrier, inc=1, device_id={"dap": lax.rem(dap + k, n)}, device_id_type=MESH
+        )
+    for k in range(1, m):
+        pl.semaphore_signal(
+            barrier, inc=1, device_id=at(lax.rem(place + k, m)), device_id_type=MESH
+        )
+    pl.semaphore_wait(barrier, n + m - 2)
+
+    across = (1 - branch) * tiles + tile
+    beside = branch * tiles + (1 - tile)
+    beyond = (1 - branch) * tiles + (1 - tile)
+    to_tile, to_branch = at(beside), at(across)
+    parts = kv_send.shape[1]
+    step_lines = lines // parts
+
+    def kv_copy(g, q, slot, device, src=None):
+        piece = kv.at[g, pl.ds(q * step_lines, step_lines)]
+        return pltpu.make_async_remote_copy(
+            src_ref=piece if src is None else src.at[pl.ds(q * step_lines, step_lines)],
+            dst_ref=piece,
+            send_sem=kv_send.at[slot, q],
+            recv_sem=kv_recv.at[slot, q],
+            device_id=device,
+            device_id_type=MESH,
+        )
+
+    waits = []
+    for q in range(parts):
+        for slot, device in ((0, to_tile), (1, to_branch)):
+            copy = kv_copy(place, q, slot, device, own_kv)
+            copy.start()
+            waits.append(copy)
+    small = []
+    for k in range(1, m):
+        small.append(
+            start_remote(
+                own_mask, mask.at[place], mask_send.at[k - 1], mask_recv.at[k - 1],
+                at(lax.rem(place + k, m)),
+            )
+        )
+    for k in range(1, n):
+        small.append(
+            start_remote(
+                own_bias, bias.at[dap], bias_send.at[k - 1], bias_recv.at[k - 1],
+                {"dap": lax.rem(dap + k, n)},
+            )
+        )
+    kv[place] = own_kv[...]
+    bias[dap] = own_bias[...]
+    mask[place] = own_mask[...]
+    for copy in small:
+        copy.wait()
+
+    for g in range(0, m, 2):
+        lower = lax.broadcasted_iota(jnp.int32, (lines, LANES), 1) < half
+        both = jnp.where(lower, mask[g], pltpu.roll(mask[g + 1], half, 1))
+        mask_wide[:, (g // 2) * LANES : (g // 2 + 1) * LANES] = (both - 1.0) * mask_big
+    for g in range(0, n, 2):
+        for h in range(heads):
+            first = bias[g, h].astype(jnp.float32)
+            second = bias[g + 1, h].astype(jnp.float32)
+            lower = lax.broadcasted_iota(jnp.int32, first.shape, 1) < half
+            top = jnp.where(lower, first, pltpu.roll(second, half, 1))
+            bottom = jnp.where(lower, pltpu.roll(first, half, 1), second)
+            bias_wide[h * sites : (h + 1) * sites, (g // 2) * LANES : (g // 2 + 1) * LANES] = (
+                jnp.concatenate([top, bottom], axis=0)
+            )
+
+    head_width = width // heads
+    head_of = lax.broadcasted_iota(jnp.int32, (sites, width), 1) // head_width
+
+    def attend(line):
+        asked = query[line]
+        stacked = jnp.concatenate(
+            [jnp.where(head_of == h, asked, jnp.zeros_like(asked)) for h in range(heads)], axis=0
+        )
+        pairs = kv[:, line].reshape(m * sites, 2 * width)
+        scores = lax.dot_general(
+            stacked, pairs[:, :width], (((1,), (1,)), ((), ())), preferred_element_type=jnp.float32
+        )
+        scores = scores + bias_wide[...] + mask_wide[line : line + 1]
+        weights = jnp.exp(scores - jnp.max(scores, axis=1, keepdims=True))
+        row_sum = jnp.sum(weights, axis=1, keepdims=True)
+        found = (
+            jnp.dot(
+                weights.astype(jnp.bfloat16), pairs[:, width:], preferred_element_type=jnp.float32
+            )
+            / row_sum
+        )
+        joined = jnp.zeros((sites, width), jnp.float32)
+        for h in range(heads):
+            joined = jnp.where(head_of == h, found[h * sites : (h + 1) * sites], joined)
+        out[line] = joined
+
+    def finish_part(q):
+        kv_copy(across, q, 1, to_branch).wait_recv()
+        kv_copy(beyond, q, 2, to_branch).wait_recv()
+        for line in range(q * step_lines, (q + 1) * step_lines):
+            attend(line)
+
+    for q in range(parts):
+        kv_copy(beside, q, 0, to_tile).wait_recv()
+        copy = kv_copy(beside, q, 2, to_branch)
+        copy.start()
+        waits.append(copy)
+        if q:
+            finish_part(q - 1)
+    finish_part(parts - 1)
+    for copy in waits:
+        copy.wait_send()
+
+
+def fused_attention(query, kv, bias, mask, heads):
+    lines, sites, width = query.shape
+    n, m, parts = lax.axis_size("dap"), lax.axis_size(("branch", "tile")), 4
+    vmem = pl.BlockSpec(memory_space=pltpu.VMEM)
+    dma = pltpu.SemaphoreType.DMA
+    return pl.pallas_call(
+        functools.partial(attention_kernel, heads),
+        out_shape=jax.ShapeDtypeStruct(query.shape, jnp.float32),
+        in_specs=[vmem] * 4,
+        out_specs=vmem,
+        scratch_shapes=[
+            pltpu.VMEM((m, *kv.shape), jnp.bfloat16),
+            pltpu.VMEM((n, *bias.shape), jnp.bfloat16),
+            pltpu.VMEM((m, *mask.shape), jnp.float32),
+            pltpu.VMEM((heads * sites, m * sites), jnp.float32),
+            pltpu.VMEM((lines, m * sites), jnp.float32),
+            dma((3, parts)), dma((3, parts)),
+            dma((n - 1,)), dma((n - 1,)), dma((m - 1,)), dma((m - 1,)),
+        ],
+        compiler_params=pltpu.CompilerParams(
+            collective_id=2, has_side_effects=True, vmem_limit_bytes=32 * 1024 * 1024
+        ),
+        cost_estimate=pl.CostEstimate(
+            flops=4 * lines * heads * sites * m * sites * width,
+            bytes_accessed=4 << 20,
+            transcendentals=lines * heads * sites * m * sites,
+        ),
+        name="attention",
+    )(query, kv, bias, mask)
+
+
+def factor_kernel(
+    left, right, left_all, right_all, left_got, right_got,
+    left_send, left_recv, right_send, right_recv,
+):
+    tiles = lax.axis_size("tile")
+    n = left_got.shape[0]
+    dap = lax.axis_index("dap")
+    block = lax.axis_index("branch") * tiles + lax.axis_index("tile")
+
+    def at(index, column):
+        return {"branch": index // tiles, "tile": lax.rem(index, tiles), "dap": column}
+
+    def others(index, column):
+        return jnp.logical_or(index != block, column != dap)
+
+    barrier = pltpu.get_barrier_semaphore()
+    for k in range(1, n * n):
+        peer = lax.rem(block * n + dap + k, n * n)
+        pl.semaphore_signal(
+            barrier, inc=1, device_id=at(peer // n, lax.rem(peer, n)), device_id_type=MESH
+        )
+    pl.semaphore_wait(barrier, n * n - 1)
+
+    copies = [
+        start_remote(
+            left, left_got.at[dap], left_send.at[k - 1], left_recv.at[k - 1],
+            {"dap": lax.rem(dap + k, n)},
+        )
+        for k in range(1, n)
+    ]
+
+    def right_copy(slot, index, column, k):
+        return pltpu.make_async_remote_copy(
+            src_ref=right,
+            dst_ref=right_got.at[slot],
+            send_sem=right_send.at[k],
+            recv_sem=right_recv.at[slot],
+            device_id=at(index, column),
+            device_id_type=MESH,
+        )
+
+    for k in range(n):
+
+        @pl.when(others(k, block))
+        def _(k=k):
+            right_copy(dap, k, block, k).start()
+
+    left_got[dap] = left[...]
+
+    @pl.when(dap == block)
+    def _():
+        right_got[dap] = right[...]
+
+    for copy in copies:
+        copy.wait()
+    for k in range(n):
+
+        @pl.when(others(dap, k))
+        def _(k=k):
+            right_copy(k, dap, k, k).wait_recv()
+
+        @pl.when(others(k, block))
+        def _(k=k):
+            right_copy(dap, k, block, k).wait_send()
+
+    left_all[...] = left_got[...]
+    right_all[...] = right_got[...]
+
+
+def trade_factors(left, right):
+    n = lax.axis_size("dap")
+    vmem = pl.BlockSpec(memory_space=pltpu.VMEM)
+    dma = pltpu.SemaphoreType.DMA
+    shape = (n, *left.shape)
+    return pl.pallas_call(
+        factor_kernel,
+        out_shape=[jax.ShapeDtypeStruct(shape, jnp.bfloat16)] * 2,
+        in_specs=[vmem] * 2,
+        out_specs=[vmem] * 2,
+        scratch_shapes=[
+            pltpu.VMEM(shape, jnp.bfloat16),
+            pltpu.VMEM(shape, jnp.bfloat16),
+            dma((n - 1,)), dma((n - 1,)), dma((n,)), dma((n,)),
+        ],
+        compiler_params=pltpu.CompilerParams(collective_id=3, has_side_effects=True),
+        cost_estimate=pl.CostEstimate(flops=0, bytes_accessed=1 << 20, transcendentals=0),
+        name="factors",
+    )(left, right)
+
+
 def body(
     homolog_hidden,
     duo_hidden,
@@ -446,6 +696,11 @@
     lines_each_shard, sites_each_shard, lineup_feature_extent = homolog_hidden.shape
     columns_per_device = duo_hidden.shape[1]
     number_of_heads = duo_logit_projector.shape[1]
+    square = (
+        duo_hidden.shape[:2] == (LANES // 2, LANES // 2)
+        and lax.axis_size("branch") == lax.axis_size("tile") == 2
+        and lax.axis_size("dap") == 4
+    )
     head_channels = lineup_feature_extent // number_of_heads
     outer_channels = dyadic_factor_projector.shape[1] // 2
     row_start = lax.axis_index(("branch", "tile")) * sites_each_shard
@@ -464,19 +719,6 @@
         "ijb,bc->ijc", one_hot, separation_bin_vectors, preferred_element_type=jnp.float32
     )
     pair_normed = standardize_features(duo_hidden_values, duo_logit_rescale, 2).astype(jnp.bfloat16)
-    local_bias = jnp.einsum(
-        "ijc,ch->hij", pair_normed, duo_logit_projector, preferred_element_type=jnp.float32
-    ).astype(jnp.bfloat16)
-    row_bias = lax.all_gather(
-        local_bias.reshape(number_of_heads, sites_each_shard * columns_per_device), "dap", axis=0
-    ).reshape(-1, number_of_heads, sites_each_shard, columns_per_device)
-    row_bias = jnp.transpose(row_bias, (1, 2, 0, 3)).reshape(number_of_heads, sites_each_shard, -1)
-    mask_grid = lax.all_gather(
-        homolog_valid_flags.astype(jnp.bfloat16), ("dap", "branch", "tile"), axis=0
-    ).reshape(lax.axis_size("dap"), -1, lines_each_shard, sites_each_shard)
-    mask_grid = jnp.transpose(mask_grid, (0, 2, 1, 3)).reshape(
-        lax.axis_size("dap") * lines_each_shard, -1
-    )
     lineup_standardized = standardize_features(homolog_hidden, homolog_heeded_rescale, 2).astype(
         jnp.bfloat16
     )
@@ -493,46 +735,78 @@
         ..., lineup_feature_extent : 3 * lineup_feature_extent
     ].astype(jnp.bfloat16)
     sigmoid_switches = jax.nn.sigmoid(mapped_contents[..., 3 * lineup_feature_extent :])
-    run_max = jnp.full((lines_each_shard, number_of_heads, sites_each_shard), -jnp.inf, jnp.float32)
-    run_sum = jnp.zeros((lines_each_shard, number_of_heads, sites_each_shard), jnp.float32)
-    run_acc = jnp.zeros(
-        (lines_each_shard, number_of_heads, sites_each_shard, head_channels), jnp.float32
-    )
-    key_value_slice = lax.all_gather(key_value_pairs, ("branch", "tile"), axis=1, tiled=True)
-    mask_piece = lax.dynamic_slice_in_dim(
-        mask_grid, lax.axis_index("dap") * lines_each_shard, lines_each_shard, axis=0
-    )
-    slice_length = key_value_slice.shape[1]
-    key_per_head = key_value_slice[..., :lineup_feature_extent].reshape(
-        lines_each_shard, slice_length, number_of_heads, head_channels
-    )
-    value_per_head = key_value_slice[..., lineup_feature_extent:].reshape(
-        lines_each_shard, slice_length, number_of_heads, head_channels
-    )
-    key_bias = row_bias.astype(jnp.float32)
-    scores = jnp.einsum(
-        "sihd,sjhd->shij", asking_array, key_per_head, preferred_element_type=jnp.float32
-    )
-    scores = (
-        scores
-        + key_bias[None]
-        + ((mask_piece.astype(jnp.float32) - 1.0) * mask_big)[:, None, None, :]
-    )
-    new_max = jnp.max(scores, axis=-1)
-    old_scale = jnp.exp(run_max - new_max)
-    weights = jnp.exp(scores - new_max[..., None])
-    run_sum = run_sum * old_scale + jnp.sum(weights, axis=-1)
-    run_acc = run_acc * old_scale[..., None] + jnp.einsum(
-        "shij,sjhd->shid",
-        weights.astype(jnp.bfloat16),
-        value_per_head,
-        preferred_element_type=jnp.float32,
-    )
-    run_max, run_sum, run_acc = (new_max, run_sum, run_acc)
-    focused_readout = run_acc / run_sum[..., None]
-    focused_readout = jnp.transpose(focused_readout, (0, 2, 1, 3)).reshape(
-        lines_each_shard, sites_each_shard, lineup_feature_extent
-    )
+    if square:
+        pairs = sites_each_shard // 2
+        pair_order = pair_normed.reshape(2, pairs, columns_per_device, -1).transpose(1, 0, 2, 3)
+        local_bias = jnp.einsum(
+            "tpc,ch->htp",
+            pair_order.reshape(pairs, LANES, -1),
+            duo_logit_projector,
+            preferred_element_type=jnp.float32,
+        ).astype(jnp.bfloat16)
+        focused_readout = fused_attention(
+            asking_array.reshape(homolog_hidden.shape),
+            key_value_pairs,
+            local_bias,
+            jnp.pad(
+                homolog_valid_flags.astype(jnp.float32), ((0, 0), (0, LANES - sites_each_shard))
+            ),
+            number_of_heads,
+        )
+    else:
+        local_bias = jnp.einsum(
+            "ijc,ch->hij", pair_normed, duo_logit_projector, preferred_element_type=jnp.float32
+        ).astype(jnp.bfloat16)
+        row_bias = lax.all_gather(
+            local_bias.reshape(number_of_heads, sites_each_shard * columns_per_device), "dap", axis=0
+        ).reshape(-1, number_of_heads, sites_each_shard, columns_per_device)
+        row_bias = jnp.transpose(row_bias, (1, 2, 0, 3)).reshape(number_of_heads, sites_each_shard, -1)
+        mask_grid = lax.all_gather(
+            homolog_valid_flags.astype(jnp.bfloat16), ("dap", "branch", "tile"), axis=0
+        ).reshape(lax.axis_size("dap"), -1, lines_each_shard, sites_each_shard)
+        mask_grid = jnp.transpose(mask_grid, (0, 2, 1, 3)).reshape(
+            lax.axis_size("dap") * lines_each_shard, -1
+        )
+        run_max = jnp.full((lines_each_shard, number_of_heads, sites_each_shard), -jnp.inf, jnp.float32)
+        run_sum = jnp.zeros((lines_each_shard, number_of_heads, sites_each_shard), jnp.float32)
+        run_acc = jnp.zeros(
+            (lines_each_shard, number_of_heads, sites_each_shard, head_channels), jnp.float32
+        )
+        key_value_slice = lax.all_gather(key_value_pairs, ("branch", "tile"), axis=1, tiled=True)
+        mask_piece = lax.dynamic_slice_in_dim(
+            mask_grid, lax.axis_index("dap") * lines_each_shard, lines_each_shard, axis=0
+        )
+        slice_length = key_value_slice.shape[1]
+        key_per_head = key_value_slice[..., :lineup_feature_extent].reshape(
+            lines_each_shard, slice_length, number_of_heads, head_channels
+        )
+        value_per_head = key_value_slice[..., lineup_feature_extent:].reshape(
+            lines_each_shard, slice_length, number_of_heads, head_channels
+        )
+        key_bias = row_bias.astype(jnp.float32)
+        scores = jnp.einsum(
+            "sihd,sjhd->shij", asking_array, key_per_head, preferred_element_type=jnp.float32
+        )
+        scores = (
+            scores
+            + key_bias[None]
+            + ((mask_piece.astype(jnp.float32) - 1.0) * mask_big)[:, None, None, :]
+        )
+        new_max = jnp.max(scores, axis=-1)
+        old_scale = jnp.exp(run_max - new_max)
+        weights = jnp.exp(scores - new_max[..., None])
+        run_sum = run_sum * old_scale + jnp.sum(weights, axis=-1)
+        run_acc = run_acc * old_scale[..., None] + jnp.einsum(
+            "shij,sjhd->shid",
+            weights.astype(jnp.bfloat16),
+            value_per_head,
+            preferred_element_type=jnp.float32,
+        )
+        run_max, run_sum, run_acc = (new_max, run_sum, run_acc)
+        focused_readout = run_acc / run_sum[..., None]
+        focused_readout = jnp.transpose(focused_readout, (0, 2, 1, 3)).reshape(
+            lines_each_shard, sites_each_shard, lineup_feature_extent
+        )
     merged_focus_groups = (sigmoid_switches * focused_readout).astype(jnp.bfloat16)
     lineup_updated_state = (
         homolog_hidden.astype(jnp.float32)
@@ -546,46 +820,74 @@
     outer_product_normalized = standardize_features(lineup_updated_state, dyadic_rescale, 2).astype(
         jnp.bfloat16
     )
-    factors = (
-        jnp.einsum(
-            "ezp,pb->ezb",
-            outer_product_normalized,
-            dyadic_factor_projector,
-            preferred_element_type=jnp.float32,
-        )
-        * homolog_valid_flags.astype(jnp.float32)[..., None]
-    )
-    factors = factors.astype(jnp.bfloat16)
-    all_factors = lax.all_gather(factors, ("dap", "branch", "tile"), axis=0).reshape(
-        lax.axis_size("dap"), -1, lines_each_shard, sites_each_shard, 2 * outer_channels
-    )
-    alignment_rows = mask_grid.shape[0]
-    left_rows = lax.dynamic_index_in_dim(
-        all_factors, lax.axis_index(("branch", "tile")), axis=1, keepdims=False
-    )[..., :outer_channels].reshape(alignment_rows, sites_each_shard, outer_channels)
-    block = col_start // sites_each_shard
-    right_rows = lax.dynamic_index_in_dim(all_factors, block, axis=1, keepdims=False)[
-        ..., outer_channels:
-    ].reshape(alignment_rows, sites_each_shard, outer_channels)
-    right_rows = lax.dynamic_slice_in_dim(
-        right_rows, col_start - block * sites_each_shard, columns_per_device, axis=1
-    )
-    mask_rows = lax.dynamic_slice_in_dim(mask_grid, row_start, sites_each_shard, axis=1)
-    mask_right = lax.dynamic_slice_in_dim(mask_grid, col_start, columns_per_device, axis=1)
-    counts = jnp.einsum("si,sj->ij", mask_rows, mask_right, preferred_element_type=jnp.float32)
     exit_by_channel = dyadic_exit_projector.reshape(outer_channels, outer_channels, -1)
-    spread_right = jnp.einsum(
-        "sjd,cdz->scjz", right_rows, exit_by_channel, preferred_element_type=jnp.float32
-    ).astype(jnp.bfloat16)
-    update = jnp.einsum(
-        "sic,scjz->ijz", left_rows, spread_right, preferred_element_type=jnp.float32
-    )
+    if square:
+        flag_row = homolog_valid_flags.reshape(1, -1).astype(jnp.float32)
+        factors = (
+            jnp.einsum(
+                "ep,pb->be",
+                outer_product_normalized.reshape(-1, lineup_feature_extent),
+                dyadic_factor_projector,
+                preferred_element_type=jnp.float32,
+            )
+            * flag_row
+        ).astype(jnp.bfloat16)
+        flag_rows = jnp.broadcast_to(flag_row, (16, flag_row.shape[1])).astype(jnp.bfloat16)
+        traded = trade_factors(
+            jnp.concatenate([factors[:outer_channels], flag_rows]),
+            jnp.concatenate([factors[outer_channels:], flag_rows]),
+        )
+        left_rows, right_rows = (
+            part[:, :outer_channels].reshape(
+                -1, outer_channels, lines_each_shard, sites_each_shard
+            )
+            for part in traded
+        )
+        mask_rows, mask_right = (
+            part[:, outer_channels].reshape(-1, sites_each_shard) for part in traded
+        )
+        counts = jnp.einsum("si,sj->ij", mask_rows, mask_right, preferred_element_type=jnp.float32)
+        spread_right = jnp.einsum(
+            "gdsj,cdz->gscjz", right_rows, exit_by_channel, preferred_element_type=jnp.float32
+        ).astype(jnp.bfloat16)
+        update = jnp.einsum(
+            "gcsi,gscjz->ijz", left_rows, spread_right, preferred_element_type=jnp.float32
+        )
+    else:
+        factors = (
+            jnp.einsum(
+                "ezp,pb->ezb",
+                outer_product_normalized,
+                dyadic_factor_projector,
+                preferred_element_type=jnp.float32,
+            )
+            * homolog_valid_flags.astype(jnp.float32)[..., None]
+        )
+        factors = factors.astype(jnp.bfloat16)
+        all_factors = lax.all_gather(factors, ("dap", "branch", "tile"), axis=0).reshape(
+            lax.axis_size("dap"), -1, lines_each_shard, sites_each_shard, 2 * outer_channels
+        )
+        alignment_rows = mask_grid.shape[0]
+        left_rows = lax.dynamic_index_in_dim(
+            all_factors, lax.axis_index(("branch", "tile")), axis=1, keepdims=False
+        )[..., :outer_channels].reshape(alignment_rows, sites_each_shard, outer_channels)
+        block = col_start // sites_each_shard
+        right_rows = lax.dynamic_index_in_dim(all_factors, block, axis=1, keepdims=False)[
+            ..., outer_channels:
+        ].reshape(alignment_rows, sites_each_shard, outer_channels)
+        right_rows = lax.dynamic_slice_in_dim(
+            right_rows, col_start - block * sites_each_shard, columns_per_device, axis=1
+        )
+        mask_rows = lax.dynamic_slice_in_dim(mask_grid, row_start, sites_each_shard, axis=1)
+        mask_right = lax.dynamic_slice_in_dim(mask_grid, col_start, columns_per_device, axis=1)
+        counts = jnp.einsum("si,sj->ij", mask_rows, mask_right, preferred_element_type=jnp.float32)
+        spread_right = jnp.einsum(
+            "sjd,cdz->scjz", right_rows, exit_by_channel, preferred_element_type=jnp.float32
+        ).astype(jnp.bfloat16)
+        update = jnp.einsum(
+            "sic,scjz->ijz", left_rows, spread_right, preferred_element_type=jnp.float32
+        )
     duo_hidden_values = duo_hidden_values + update / (count_eps + counts)[..., None]
-    square = (
-        duo_hidden.shape[:2] == (LANES // 2, LANES // 2)
-        and lax.axis_size("branch") == lax.axis_size("tile") == 2
-        and lax.axis_size("dap") == 4
-    )
     for threefold_module in range(2):
         parameters = (
             triad_entry_rescales[threefold_module],

time: 345 us -> 296 us (0.86)
  blocking collectives: 45.7 us -> 0 us
  Pallas kernels: 175 us -> 212 us
  waiting for transfers between devices: 35.8 us -> 0 us
  between operations: 14.6 us -> 1.25 us
  local copies, waits for them, and re-layouts: 26.9 us -> 18.2 us
  matrix products: 27.9 us -> 36.5 us
  other arithmetic: 18.8 us -> 26.7 us
    all_gather x2 -> x0, blocking collectives: 45.7 us -> none  [the longest x1 30.1 us: body(): lax.all_gather(homolog_valid_flags.astype(jnp.bfloat16), ('dap', 'branch'...]
    all_gather x2 -> x0, waiting for transfers between devices: 35.8 us -> none  [the longest x1 35.8 us: body(): lax.all_gather(factors, ('dap', 'branch', 'tile'), axis=0)]
    pallas_call x0 -> x2, Pallas kernels: none -> 34.6 us  [the longest x1 23.2 us: fused_attention(): pl.pallas_call(functools.partial(attention_kernel, heads), out_shape=jax....]
    unnamed x35 -> x63, local copies, waits for them, and re-layouts: 2.11 us -> 13.5 us
    slice x5, local copies, waits for them, and re-layouts: 9.71 us -> 2.51 us  [the longest x2 1.58 us: body(): part[:, outer_channels].reshape(-1, sites_each_shard)]
    convert_element_type x5 -> x1, local copies, waits for them, and re-layouts: 7.25 us -> 0.08 us  [body(): flag_row = homolog_valid_flags.reshape(1, -1).astype(jnp.float32)]
    dot_general x2, matrix products: 2.58 us -> 9.05 us  [fused_update(): jnp.einsum('tpc,cd->tdp', positions.reshape(pairs, LANES, width), w_in, p...]
    convert_element_type x1, other arithmetic: 1.19 us -> 5.99 us  [fused_update(): right = (jax.nn.sigmoid(blocks[3]) * blocks[2] * flags).astype(jnp.bfloat16)]
  transfers between devices with their start and end apart: 2 -> 0, of which waited for: 1 -> 0; matrix products, arithmetic and copies ran while one was open for 5% -> 0% of each run, Pallas kernels for 0% -> 0%
where the time goes in v3:
time: 296 us; the launch traced here: 295 us
  Pallas kernels  212 us (72%)
  matrix products  36.5 us (12%)
  other arithmetic  26.7 us (9%)
  local copies, waits for them, and re-layouts  18.2 us (6%)
    pallas_call x2, Pallas kernels, fused_update(): pl.pallas_call(functools.partial(triangle_kernel, incoming), out_shape=ja...  178 us
    pallas_call x1, Pallas kernels, fused_attention(): pl.pallas_call(functools.partial(attention_kernel, heads), out_shape=jax....  23.2 us
    unnamed x63, local copies, waits for them, and re-layouts  13.5 us
    dot_general x1, matrix products, body(): jnp.einsum('gcsi,gscjz->ijz', left_rows, spread_right, preferred_element_...  13.1 us
    pallas_call x1, Pallas kernels, trade_factors(): pl.pallas_call(factor_kernel, out_shape=[jax.ShapeDtypeStruct(shape, jnp....  11.3 us
    dot_general x2, matrix products, fused_update(): jnp.einsum('tpc,cd->tdp', positions.reshape(pairs, LANES, width), w_in, p...  9.05 us
    dot_general x1, matrix products, body(): jnp.einsum('gdsj,cdz->gscjz', right_rows, exit_by_channel, preferred_elem...  8.32 us
    convert_element_type x1, other arithmetic, fused_update(): right = (jax.nn.sigmoid(blocks[3]) * blocks[2] * flags).astype(jnp.bfloat16)  5.99 us

profile of v3, /device:TPU:0, one launch (start us, length us, event | category | flops | bytes accessed | tf_op | source)
XLA Modules:
  0.0 294.8 jit_solution(15724901100574434125)
XLA Ops:
  0.6 1.1 convert_reduce_fusion
  1.8 1.2 fusion.35
  3.1 1.4 fusion.46
  4.6 1.3 copy-done.11
  6.2 2.3 fusion.72
  8.6 1.3 multiply_reduce_fusion.2
  9.9 1.3 multiply_convert_fusion.2
  11.9 23.2 %attention.1 = f32[8,64,256]{2,1,0:T(8,128)S(1)} custom-call(bf16[8,64,256]{2,1,0:T(8,128)(2,1)S(1)} %fusion.41.query, bf16[8,64,512]{2,1,0:T(8,128)(2,1)S(1)} %slice.212.own_kv, bf16[8,32,128]{2,1,0:T(8,128)(2,1)S(1)} %bitcast.97, f32[8,128]{1,0:T(8,128)S(1)} %pad.4.own_mask), custom_call_target="tpu_custom_call" | custom-call | flops 1073741824 | bytes 4194304 | tf_op jit(solution)/shard_map/attention/pallas_call | solution.py:558
  35.2 1.4 convert_reduce_fusion.1
  38.1 11.3 %factors.1 = (bf16[4,48,512]{2,1,0:T(8,128)(2,1)}, bf16[4,48,512]{2,1,0:T(8,128)(2,1)}) custom-call(bf16[48,512]{1,0:T(8,128)(2,1)} %get-tuple-element.21.left, bf16[48,512]{1,0:T(8,128)(2,1)} %get-tuple-element.20.right), custom_call_target="tpu_custom_call" | custom-call | bytes 1048576 | tf_op jit(solution)/shard_map/factors/pallas_call | solution.py:658
  52.5 8.3 %convert_bitcast_fusion = bf16[4,8,32,64,128]{4,3,2,1,0:T(8,128)(2,1)} fusion(bf16[32,32,128,1,1]{2,1,0,4,3:T(8,128)(2,1)S(1)} %bitcast.104, bf16[4,32,8,64,1]{3,2,1,0,4:T(8,128)(2,1)S(1)} %bitcast.102), kind=kOutput, calls=%fused_computation.2 | convolution fusion | flops 545259520 | bytes 17170432 | tf_op jit(solution)/shard_map/gdsj,cdz->gscjz/dot_general | solution.py:850
  61.0 13.1 %fusion.24 = f32[64,64,128]{2,0,1:T(8,128)S(1)} fusion(bf16[4,8,32,64,128]{4,3,2,1,0:T(8,128)(2,1)} %convert_bitcast_fusion, bf16[4,32,8,64]{3,2,1,0:T(8,128)(2,1)S(1)} %reshape.179), kind=kOutput, calls=%fused_computation.44 | convolution fusion | flops 1073741824 | bytes 19005440 | tf_op jit(solution)/shard_map/gcsi,gscjz->ijz/dot_general | solution.py:853
  74.2 2.8 fusion.67
  77.0 1.3 multiply_reduce_fusion.1
  78.4 1.3 multiply_convert_fusion.1.normed
  80.7 4.5 %convolution_bitcast_fusion.1 = f32[32,512,128]{2,1,0:T(8,128)} fusion(bf16[32,128,128]{2,1,0:T(8,128)(2,1)S(1)} %bitcast.98, bf16[2,128,512]{2,1,0:T(8,128)(2,1)S(1)} %copy-done.15), kind=kOutput, calls=%fused_computation.4 | convolution fusion | flops 536870912 | bytes 9568256 | tf_op jit(solution)/shard_map/tpc,cd->tdp/dot_general | solution.py:378
  85.4 6.0 %fusion.13 = (bf16[32,128,128]{2,1,0:T(8,128)(2,1)}, bf16[32,128,128]{2,1,0:T(8,128)(2,1)}) fusion(f32[32,512,128]{2,1,0:T(8,128)} %convolution_bitcast_fusion.1, f32[32,128]{1,0:T(8,128)S(1)} %mul.200), kind=kLoop, calls=%fused_computation.21 | loop fusion | flops 6291456 | bytes 10502144 | tf_op jit(solution)/shard_map/convert_element_type | solution.py:386
  91.5 1.6 copy-done.2
  93.1 1.2 copy-done.4
  94.3 1.2 copy-done.7
  95.6 1.2 copy-done.8
  96.8 76.5 %triangle_out.1.state = f32[64,64,128]{2,1,0:T(8,128)S(1)} custom-call(bf16[32,128,128]{2,1,0:T(8,128)(2,1)S(1)} %copy-done.8, bf16[32,128,128]{2,1,0:T(8,128)(2,1)S(1)} %copy-done.7, f32[64,64,128]{2,1,0:T(8,128)S(1)} %copy-done.2, bf16[64,64,128]{2,1,0:T(8,128)(2,1)S(1)} %copy-done.4, bf16[128,128]{1,0:T(8,128)(2,1)S(1)} %get-tuple-element.36.w_gate, ...), custom_call_target="tpu_custom_call" | custom-call | flops 268435456 | bytes 8388608 | tf_op jit(solution)/shard_map/triangle_out/pallas_call | solution.py:391
  173.9 1.3 multiply_reduce_fusion
  175.3 1.3 multiply_convert_fusion.normed
  177.2 1.1 copy-done.5
  178.3 4.5 %convolution_bitcast_fusion = f32[32,512,128]{2,1,0:T(8,128)} fusion(bf16[32,128,128]{2,1,0:T(8,128)(2,1)S(1)} %bitcast.99, bf16[2,128,512]{2,1,0:T(8,128)(2,1)S(1)} %copy-done.15), kind=kOutput, calls=%fused_computation.3 | convolution fusion | flops 536870912 | bytes 9568256 | tf_op jit(solution)/shard_map/tpc,cd->tdp/dot_general | solution.py:378
  183.0 5.9 %fusion.3 = (bf16[32,128,128]{2,1,0:T(8,128)(2,1)}, bf16[32,128,128]{2,1,0:T(8,128)(2,1)}) fusion(f32[32,512,128]{2,1,0:T(8,128)} %convolution_bitcast_fusion, f32[32,128]{1,0:T(8,128)S(1)} %mul.212), kind=kLoop, calls=%fused_computation.7 | loop fusion | flops 6291456 | bytes 10502144 | tf_op jit(solution)/shard_map/convert_element_type | solution.py:385
  189.0 1.2 copy-done.6
  190.3 1.2 copy-done.9
  191.5 1.2 copy-done.10
  192.7 101.1 %triangle_in.1 = bf16[64,64,128]{2,1,0:T(8,128)(2,1)S(1)} custom-call(bf16[32,128,128]{2,1,0:T(8,128)(2,1)S(1)} %copy-done.10, bf16[32,128,128]{2,1,0:T(8,128)(2,1)S(1)} %copy-done.9, f32[64,64,128]{2,1,0:T(8,128)S(1)} %triangle_out.1.state, bf16[64,64,128]{2,1,0:T(8,128)(2,1)S(1)} %copy-done.6, bf16[128,128]{1,0:T(8,128)(2,1)S(1)} %get-tuple-element.37.w_gate, ...), custom_call_target="tpu_custom_call" | custom-call | flops 268435456 | bytes 8388608 | tf_op jit(solution)/shard_map/triangle_in/pallas_call | solution.py:391
  293.8 1.0 copy.98
  (103 shorter events, 8.7 us)
Async XLA Ops:
  0.6 2.4 copy-start
  3.0 2.9 copy-start.25
  3.1 2.9 copy-start.26
  3.1 3.1 %copy-start.21 = (bf16[66,128]{1,0:T(8,128)(2,1)S(1)}, bf16[66,128]{1,0:T(8,128)(2,1)}, u32[]{:S(2)}) copy-start(bf16[66,128]{1,0:T(8,128)(2,1)} %param.26) | copy-start | bytes 50692
  4.5 1.3 copy-start.11
  6.2 3.7 %copy-start.29 = (f32[128]{0:T(128)S(1)}, f32[128]{0:T(128)}, u32[]{:S(2)}) copy-start(f32[128]{0:T(128)} %param.27) | copy-start | bytes 1540
  9.9 1.4 copy-start.23
  11.2 0.7 copy-start.22
  11.7 23.5 %copy-start.12 = (bf16[8,64,256]{2,1,0:T(8,128)(2,1)S(1)}, bf16[8,64,256]{2,1,0:T(8,128)(2,1)}, u32[]{:S(2)}) copy-start(bf16[8,64,256]{2,1,0:T(8,128)(2,1)} %param.20) | copy-start | bytes 786436
  11.7 23.5 %copy-start.30 = (bf16[256,256]{1,0:T(8,128)(2,1)S(1)}, bf16[256,256]{1,0:T(8,128)(2,1)}, u32[]{:S(2)}) copy-start(bf16[256,256]{1,0:T(8,128)(2,1)} %param.31) | copy-start | bytes 393220
  35.1 1.9 copy-start.24
  35.2 2.1 copy-start.20
  35.2 17.3 %copy-start.14 = (bf16[1024,128]{1,0:T(8,128)(2,1)S(1)}, bf16[1024,128]{1,0:T(8,128)(2,1)}, u32[]{:S(2)}) copy-start(bf16[1024,128]{1,0:T(8,128)(2,1)} %param.34) | copy-start | bytes 786436
  36.6 14.8 %copy-start.13 = (bf16[8,64,256]{2,1,0:T(8,128)(2,1)}, bf16[8,64,256]{2,1,0:T(8,128)(2,1)S(1)}, u32[]{:S(2)}) copy-start(bf16[8,64,256]{2,1,0:T(8,128)(2,1)S(1)} %get-tuple-element.40) | copy-start | bytes 786436
  52.5 8.3 %copy-start.16 = (bf16[4,48,512]{2,1,0:T(8,128)(2,1)S(1)}, bf16[4,48,512]{2,1,0:T(8,128)(2,1)}, u32[]{:S(2)}) copy-start(bf16[4,48,512]{2,1,0:T(8,128)(2,1)} %get-tuple-element.4) | copy-start | bytes 589828
  74.2 2.8 copy-start.27
  76.9 2.7 copy-start.1
  78.3 2.4 copy-start.15
  79.7 1.0 copy-start.3
  80.7 4.5 %copy-start.19 = (s32[64,64]{1,0:T(8,128)S(1)}, s32[64,64]{1,0:T(8,128)}, u32[]{:S(2)}) copy-start(s32[64,64]{1,0:T(8,128)} %param.23) | copy-start | bytes 49156
  85.4 6.0 %copy-start.17 = (bf16[2,128,128]{2,1,0:T(8,128)(2,1)S(1)}, bf16[2,128,128]{2,1,0:T(8,128)(2,1)}, u32[]{:S(2)}) copy-start(bf16[2,128,128]{2,1,0:T(8,128)(2,1)} %param.39) | copy-start | bytes 196612
  85.4 6.0 %copy-start.18 = (bf16[2,128,128]{2,1,0:T(8,128)(2,1)S(1)}, bf16[2,128,128]{2,1,0:T(8,128)(2,1)}, u32[]{:S(2)}) copy-start(bf16[2,128,128]{2,1,0:T(8,128)(2,1)} %param.37) | copy-start | bytes 196612
  85.4 6.0 %copy-start.28 = (f32[2,128]{1,0:T(2,128)S(1)}, f32[2,128]{1,0:T(2,128)}, u32[]{:S(2)}) copy-start(f32[2,128]{1,0:T(2,128)} %param.38) | copy-start | bytes 3076
  91.5 1.6 copy-start.2
  93.1 1.2 copy-start.4
  94.3 1.2 copy-start.7
  95.6 1.2 copy-start.8
  177.2 1.1 copy-start.5
  189.0 1.2 copy-start.6
  190.3 1.2 copy-start.9
  191.5 1.2 copy-start.10

commit v4 on v3

--- a/solution.py
+++ b/solution.py
@@ -103,14 +103,18 @@
 
 def triangle_kernel(
     incoming,
-    own_in,
-    spread_in,
     state,
-    normed,
+    flags,
+    norm_gain,
+    w_own,
+    w_spread,
     w_gate,
     out_gain,
     w_out,
     out,
+    own_in,
+    spread_in,
+    normed,
     own,
     spread,
     own_wide,
@@ -153,13 +157,50 @@
         pl.semaphore_signal(
             barrier, inc=1, device_id=spread_to(lax.rem(place + k, m)), device_id_type=MESH
         )
-    pl.semaphore_wait(barrier, n + m - 2)
+    rows, cols, width = state.shape
+
+    def normalise(i, _):
+        values = state[i]
+        centred = values - jnp.mean(values, axis=1, keepdims=True)
+        spread_of = jnp.mean(centred * centred, axis=1, keepdims=True)
+        normed[pl.ds(pl.multiple_of(i * cols, cols), cols), :] = (
+            centred * lax.rsqrt(spread_of + norm_eps) * norm_gain[...]
+        )
+        return 0
+
+    lax.fori_loop(0, rows, normalise, 0, unroll=4)
+
+    def project(weights, factor):
+        def step(t, _):
+            if incoming:
+                chosen = [normed[pl.ds(t + part * pairs, rows, stride=cols), :] for part in (0, 1)]
+            else:
+                chosen = [
+                    normed[pl.ds(pl.multiple_of((t + part * pairs) * cols, cols), cols), :]
+                    for part in (0, 1)
+                ]
+            mapped = lax.dot_general(
+                weights[...],
+                jnp.concatenate(chosen, axis=0).astype(jnp.bfloat16),
+                (((1,), (1,)), ((), ())),
+                preferred_element_type=jnp.float32,
+            )
+            factor[t] = (jax.nn.sigmoid(mapped[width:]) * mapped[:width] * flags[t]).astype(
+                jnp.bfloat16
+            )
+            return 0
+
+        lax.fori_loop(0, pairs, step, 0, unroll=2)
 
     def channels(ref, index):
         return ref.at[:, pl.ds(pl.multiple_of(index * share, share), share), :]
 
     trades = [[], []]
-    for which, (src, dst) in enumerate(((spread_in, spread.at[place, me]), (own_in, own.at[me]))):
+    plans = ((w_spread, spread_in, spread.at[place, me]), (w_own, own_in, own.at[me]))
+    for which, (weights, src, dst) in enumerate(plans):
+        project(weights, src)
+        if which == 0:
+            pl.semaphore_wait(barrier, n + m - 2)
         for k in range(1, n):
             to = lax.rem(me + k, n)
             trades[which].append(
@@ -266,20 +307,20 @@
         finish_own()
         multiply(place)
         for h in range(1, m):
-            for side, sign, to, there in sides:
-                g = place - sign * h
-                has_block = (g >= 0) if sign > 0 else (g < m)
-
-                @pl.when(has_block)
-                def _(side=side, to=to, there=there, g=g, h=h):
-                    for k in range(n):
+            for k in range(n):
+                for side, sign, to, there in sides:
+                    g = place - sign * h
+                    has_block = (g >= 0) if sign > 0 else (g < m)
+
+                    @pl.when(has_block)
+                    def _(side=side, to=to, there=there, g=g, h=h, k=k):
                         spread_copy(
                             g, k, side * (m - 1) + h - 1, spread_to(lax.rem(place + 1, m))
                         ).wait_recv()
                         if h < m - 1:
 
                             @pl.when(there)
-                            def _(k=k):
+                            def _():
                                 spread_copy(g, k, side * (m - 1) + h, spread_to(to)).start()
 
             for side, sign, to, there in sides:
@@ -354,7 +395,11 @@
         for part in range(2):
             i = part * pairs + t
             gate = jax.nn.sigmoid(
-                jnp.dot(normed[i], w_gate[...], preferred_element_type=jnp.float32)
+                jnp.dot(
+                    normed[pl.ds(pl.multiple_of(i * cols, cols), cols), :].astype(jnp.bfloat16),
+                    w_gate[...],
+                    preferred_element_type=jnp.float32,
+                )
             )
             out[i] = (state[i] + gate * update[part * half : (part + 1) * half]).astype(out.dtype)
         return 0
@@ -368,22 +413,12 @@
     width = w_in.shape[1] // 4
     rows, cols = flags.shape
     n = lax.axis_size("dap")
-    share, pairs, half = width // n, rows // 2, rows
-    normed = standardize_features(state, norm_gain, 2).astype(jnp.bfloat16)
+    share, pairs = width // n, rows // 2
     flags = flags.astype(jnp.float32)
-    positions = jnp.transpose(normed, (1, 0, 2)) if incoming else normed
-    flags = flags.T if incoming else flags
-    positions = positions.reshape(2, pairs, half, width).transpose(1, 0, 2, 3)
-    flags = flags.reshape(2, pairs, half).transpose(1, 0, 2).reshape(pairs, 1, LANES)
-    mapped = jnp.einsum(
-        "tpc,cd->tdp",
-        positions.reshape(pairs, LANES, width),
-        w_in,
-        preferred_element_type=jnp.float32,
-    )
-    blocks = [mapped[:, q * width : (q + 1) * width] for q in range(4)]
-    left = (jax.nn.sigmoid(blocks[1]) * blocks[0] * flags).astype(jnp.bfloat16)
-    right = (jax.nn.sigmoid(blocks[3]) * blocks[2] * flags).astype(jnp.bfloat16)
+    flags = (flags.T if incoming else flags).reshape(2, pairs, -1)
+    flags = flags.transpose(1, 0, 2).reshape(pairs, 1, LANES)
+    turned = w_in.T
+    left, right = turned[: 2 * width], turned[2 * width :]
     own, spread = (right, left) if incoming else (left, right)
     slots = 2 * (n - 1)
     vmem = pl.BlockSpec(memory_space=pltpu.VMEM)
@@ -391,9 +426,12 @@
     return pl.pallas_call(
         functools.partial(triangle_kernel, incoming),
         out_shape=jax.ShapeDtypeStruct(state.shape, out_type),
-        in_specs=[vmem] * 7,
+        in_specs=[vmem] * 8,
         out_specs=vmem,
         scratch_shapes=[
+            pltpu.VMEM((pairs, width, LANES), jnp.bfloat16),
+            pltpu.VMEM((pairs, width, LANES), jnp.bfloat16),
+            pltpu.VMEM((rows * cols, width), jnp.float32),
             pltpu.VMEM(factor, jnp.bfloat16),
             pltpu.VMEM((n, *factor), jnp.bfloat16),
             pltpu.VMEM((n * pairs * share, LANES), jnp.float32),
@@ -418,7 +456,16 @@
             flops=2 * 256 * rows * cols * width, bytes_accessed=8 << 20, transcendentals=0
         ),
         name="triangle_in" if incoming else "triangle_out",
-    )(own, spread, state, normed, w_gate, out_gain.reshape(width, 1), w_out)
+    )(
+        state,
+        flags,
+        norm_gain.reshape(1, width),
+        own,
+        spread,
+        w_gate,
+        out_gain.reshape(width, 1),
+        w_out,
+    )
 
 
 def attention_kernel(
@@ -838,9 +885,10 @@
             jnp.concatenate([factors[outer_channels:], flag_rows]),
         )
         left_rows, right_rows = (
-            part[:, :outer_channels].reshape(
-                -1, outer_channels, lines_each_shard, sites_each_shard
-            )
+            part[:, :outer_channels]
+            .reshape(-1, outer_channels, lines_each_shard, sites_each_shard)
+            .transpose(0, 2, 3, 1)
+            .reshape(-1, sites_each_shard, outer_channels)
             for part in traded
         )
         mask_rows, mask_right = (
@@ -848,10 +896,10 @@
         )
         counts = jnp.einsum("si,sj->ij", mask_rows, mask_right, preferred_element_type=jnp.float32)
         spread_right = jnp.einsum(
-            "gdsj,cdz->gscjz", right_rows, exit_by_channel, preferred_element_type=jnp.float32
+            "sjd,cdz->scjz", right_rows, exit_by_channel, preferred_element_type=jnp.float32
         ).astype(jnp.bfloat16)
         update = jnp.einsum(
-            "gcsi,gscjz->ijz", left_rows, spread_right, preferred_element_type=jnp.float32
+            "sic,scjz->ijz", left_rows, spread_right, preferred_element_type=jnp.float32
         )
     else:
         factors = (

time: 296 us -> 254 us (0.86)
  matrix products: 36.5 us -> 12.7 us
  other arithmetic: 26.7 us -> 7.64 us
  Pallas kernels: 212 us -> 221 us
  local copies, waits for them, and re-layouts: 18.2 us -> 10.4 us
    dot_general x4 -> x1, matrix products: 30.5 us -> 8.76 us  [body(): jnp.einsum('sic,scjz->ijz', left_rows, spread_right, preferred_element_ty...]
    convert_element_type x4 -> x0, other arithmetic: 14.4 us -> none  [the longest x1 5.99 us: fused_update(): right = (jax.nn.sigmoid(blocks[3]) * blocks[2] * flags).astype(jnp.bfloat16)]
    pallas_call x2, Pallas kernels: 178 us -> 187 us  [fused_update(): pl.pallas_call(functools.partial(triangle_kernel, incoming), out_shape=ja...]
    unnamed x63 -> x45, local copies, waits for them, and re-layouts: 13.5 us -> 4.67 us
    reduce_sum x3 -> x1, other arithmetic: 4.52 us -> 0.14 us  [standardize_features(): mean_val = jnp.mean(values, axis=norm_axis, keepdims=True)]
    reduce_sum x5 -> x3, other arithmetic: 5.42 us -> 1.85 us  [standardize_features(): spread = jnp.mean(centred * centred, axis=norm_axis, keepdims=True)]
    add x0 -> x1, other arithmetic: none -> 3.35 us  [body(): duo_hidden_values + update / (count_eps + counts)[..., None]]
where the time goes in v4:
time: 254 us; the launch traced here: 253 us
  Pallas kernels  221 us (87%)
  matrix products  12.7 us (5%)
  local copies, waits for them, and re-layouts  10.4 us (4%)
  other arithmetic  7.64 us (3%)
    pallas_call x2, Pallas kernels, fused_update(): pl.pallas_call(functools.partial(triangle_kernel, incoming), out_shape=ja...  187 us
    pallas_call x1, Pallas kernels, fused_attention(): pl.pallas_call(functools.partial(attention_kernel, heads), out_shape=jax....  23.3 us
    pallas_call x1, Pallas kernels, trade_factors(): pl.pallas_call(factor_kernel, out_shape=[jax.ShapeDtypeStruct(shape, jnp....  11.3 us
    dot_general x1, matrix products, body(): jnp.einsum('sic,scjz->ijz', left_rows, spread_right, preferred_element_ty...  8.76 us

profile of v4, /device:TPU:0, one launch (start us, length us, event | category | flops | bytes accessed | tf_op | source)
XLA Modules:
  0.0 253.4 jit_solution(5994541718717549852)
XLA Ops:
  0.7 0.9 fusion.50
  1.6 2.4 fusion.52
  4.0 1.3 multiply_reduce_fusion
  5.4 1.3 multiply_convert_fusion
  6.8 0.4 fusion.42
  7.2 0.4 copy-done.4
  7.6 0.1 convert_reduce_fusion
  7.8 0.3 fusion.18
  8.1 0.5 fusion.29
  8.8 23.3 %attention.1 = f32[8,64,256]{2,1,0:T(8,128)S(1)} custom-call(bf16[8,64,256]{2,1,0:T(8,128)(2,1)S(1)} %fusion.24.query, bf16[8,64,512]{2,1,0:T(8,128)(2,1)S(1)} %slice.126.own_kv, bf16[8,32,128]{2,1,0:T(8,128)(2,1)S(1)} %bitcast.84, f32[8,128]{1,0:T(8,128)S(1)} %pad.4.own_mask), custom_call_target="tpu_custom_call" | custom-call | flops 1073741824 | bytes 4194304 | tf_op jit(solution)/shard_map/attention/pallas_call | solution.py:605
  32.1 0.4 convert_reduce_fusion.1
  32.5 0.3 fusion.21
  32.8 0.2 fusion.23
  33.1 0.2 fusion.12
  33.3 0.6 pad_maximum_fusion
  34.0 11.3 %factors.1 = (bf16[4,48,512]{2,1,0:T(8,128)(2,1)}, bf16[4,48,512]{2,1,0:T(8,128)(2,1)}) custom-call(bf16[48,512]{1,0:T(8,128)(2,1)} %get-tuple-element.21.left, bf16[48,512]{1,0:T(8,128)(2,1)} %get-tuple-element.20.right), custom_call_target="tpu_custom_call" | custom-call | bytes 1048576 | tf_op jit(solution)/shard_map/factors/pallas_call | solution.py:705
  45.3 0.9 slice_reduce_fusion.1
  46.2 0.8 slice_reduce_fusion
  47.1 0.2 convolution_add_fusion.1
  47.3 0.9 slice.76
  48.2 0.2 reshape.151
  48.4 0.8 copy.54
  49.3 0.2 reshape.149
  49.5 8.8 %fusion.7 = f32[64,64,128]{2,0,1:T(8,128)} fusion(bf16[32,64,32,1]{2,0,3,1:T(8,128)(2,1)S(1)} %copy.54, bf16[32,32,128,1]{2,1,0,3:T(8,128)(2,1)S(1)} %bitcast.93, bf16[4,32,8,64]{3,2,1,0:T(8,128)(2,1)S(1)} %reshape.149), kind=kOutput, calls=%fused_computation.11 | convolution fusion | flops 1619001344 | bytes 2621440 | tf_op jit(solution)/shard_map/sic,scjz->ijz/dot_general | solution.py:901
  58.3 3.4 %fusion.5.state = f32[64,64,128]{2,1,0:T(8,128)S(1)} fusion(f32[64,64,128]{2,1,0:T(8,128)} %copy-done.3, f32[64,64,128]{2,0,1:T(8,128)} %fusion.7, f32[64,64]{1,0:T(8,128)S(1)} %convolution_add_fusion.1), kind=kLoop, calls=%fused_computation.5 | loop fusion | flops 1048576 | bytes 6307840 | tf_op jit(solution)/shard_map/add | solution.py:938
  61.7 0.1 copy.58
  62.2 80.7 %triangle_out.1.state = f32[64,64,128]{2,1,0:T(8,128)S(1)} custom-call(f32[64,64,128]{2,1,0:T(8,128)S(1)} %fusion.5.state, f32[32,1,128]{2,1,0:T(1,128)S(1)} %reshape.155.flags, f32[1,128]{1,0:T(1,128)S(1)} %get-tuple-element.25.norm_gain, bf16[256,128]{1,0:T(8,128)(2,1)S(1)} %get-tuple-element.11.w_own, bf16[256,128]{1,0:T(8,128)(2,1)S(1)} %get-tuple-element.10.w_spread, ...), custom_call_target="tpu_custom_call" | custom-call | flops 268435456 | bytes 8388608 | tf_op jit(solution)/shard_map/triangle_out/pallas_call | solution.py:426
  142.9 1.3 copy-done.1
  144.2 0.1 copy.59
  144.7 1.6 copy-done.2
  146.3 106.1 %triangle_in.1 = bf16[64,64,128]{2,1,0:T(8,128)(2,1)S(1)} custom-call(f32[64,64,128]{2,1,0:T(8,128)S(1)} %copy-done.2, f32[32,1,128]{2,1,0:T(1,128)S(1)} %reshape.157.flags, f32[1,128]{1,0:T(1,128)S(1)} %get-tuple-element.24.norm_gain, bf16[256,128]{1,0:T(8,128)(2,1)S(1)} %get-tuple-element.9.w_own, bf16[256,128]{1,0:T(8,128)(2,1)S(1)} %get-tuple-element.8.w_spread, ...), custom_call_target="tpu_custom_call" | custom-call | flops 268435456 | bytes 8388608 | tf_op jit(solution)/shard_map/triangle_in/pallas_call | solution.py:426
  252.4 1.0 copy.72
  (74 shorter events, 1.5 us)
Async XLA Ops:
  0.6 7.4 %copy-start = (bf16[256,1024]{1,0:T(8,128)(2,1)S(1)}, bf16[256,1024]{1,0:T(8,128)(2,1)}, u32[]{:S(2)}) copy-start(bf16[256,1024]{1,0:T(8,128)(2,1)} %param.30) | copy-start | bytes 1572868
  1.6 3.8 %copy-start.18 = (f32[128]{0:T(128)S(1)}, f32[128]{0:T(128)}, u32[]{:S(2)}) copy-start(f32[128]{0:T(128)} %param.27) | copy-start | bytes 1540
  4.0 2.7 %copy-start.3 = (f32[64,64,128]{2,1,0:T(8,128)}, f32[64,64,128]{2,1,0:T(8,128)S(1)}, u32[]{:S(2)}) copy-start(f32[64,64,128]{2,1,0:T(8,128)S(1)} %get-tuple-element.31) | copy-start | bytes 6291460
  5.4 1.4 copy-start.13
  6.7 1.0 copy-start.4
  6.7 1.4 copy-start.14
  8.1 0.7 copy-start.12
  8.8 23.3 %copy-start.20 = (bf16[256,256]{1,0:T(8,128)(2,1)S(1)}, bf16[256,256]{1,0:T(8,128)(2,1)}, u32[]{:S(2)}) copy-start(bf16[256,256]{1,0:T(8,128)(2,1)} %param.31) | copy-start | bytes 393220
  32.1 0.7 copy-start.15
  32.1 1.0 copy-start.11
  32.5 17.0 %copy-start.5 = (bf16[8,64,256]{2,1,0:T(8,128)(2,1)}, bf16[8,64,256]{2,1,0:T(8,128)(2,1)S(1)}, u32[]{:S(2)}) copy-start(bf16[8,64,256]{2,1,0:T(8,128)(2,1)S(1)} %get-tuple-element.40) | copy-start | bytes 786436
  32.8 16.7 %copy-start.19 = (bf16[1024,128]{1,0:T(8,128)(2,1)S(1)}, bf16[1024,128]{1,0:T(8,128)(2,1)}, u32[]{:S(2)}) copy-start(bf16[1024,128]{1,0:T(8,128)(2,1)} %param.34) | copy-start | bytes 786436
  45.3 4.0 %copy-start.7 = (bf16[4,48,512]{2,1,0:T(8,128)(2,1)S(1)}, bf16[4,48,512]{2,1,0:T(8,128)(2,1)}, u32[]{:S(2)}) copy-start(bf16[4,48,512]{2,1,0:T(8,128)(2,1)} %get-tuple-element.4) | copy-start | bytes 589828
  58.2 3.4 %copy-start.8 = (bf16[2,128,128]{2,1,0:T(8,128)(2,1)S(1)}, bf16[2,128,128]{2,1,0:T(8,128)(2,1)}, u32[]{:S(2)}) copy-start(bf16[2,128,128]{2,1,0:T(8,128)(2,1)} %param.39) | copy-start | bytes 196612
  58.2 3.4 %copy-start.9 = (bf16[2,128,128]{2,1,0:T(8,128)(2,1)S(1)}, bf16[2,128,128]{2,1,0:T(8,128)(2,1)}, u32[]{:S(2)}) copy-start(bf16[2,128,128]{2,1,0:T(8,128)(2,1)} %param.37) | copy-start | bytes 196612
  58.2 3.4 %copy-start.6 = (bf16[2,128,512]{2,1,0:T(8,128)(2,1)S(1)}, bf16[2,128,512]{2,1,0:T(8,128)(2,1)}, u32[]{:S(2)}) copy-start(bf16[2,128,512]{2,1,0:T(8,128)(2,1)} %param.36) | copy-start | bytes 786436
  58.2 3.6 %copy-start.10 = (s32[64,64]{1,0:T(8,128)S(1)}, s32[64,64]{1,0:T(8,128)}, u32[]{:S(2)}) copy-start(s32[64,64]{1,0:T(8,128)} %param.23) | copy-start | bytes 49156
  58.2 3.8 %copy-start.16 = (f32[2,128]{1,0:T(2,128)S(1)}, f32[2,128]{1,0:T(2,128)}, u32[]{:S(2)}) copy-start(f32[2,128]{1,0:T(2,128)} %param.38) | copy-start | bytes 3076
  58.2 3.9 %copy-start.17 = (f32[2,128]{1,0:T(2,128)S(1)}, f32[2,128]{1,0:T(2,128)}, u32[]{:S(2)}) copy-start(f32[2,128]{1,0:T(2,128)} %param.35) | copy-start | bytes 3076
  142.9 1.3 copy-start.1
  144.7 1.6 copy-start.2

commit v5 on v4

--- a/solution.py
+++ b/solution.py
@@ -253,7 +253,7 @@
             )
             return 0
 
-        lax.fori_loop(0, share, step, 0, unroll=4)
+        lax.fori_loop(0, share, step, 0, unroll=8)
         outgoing_blocks[g] = (
             product_wide[...].reshape(pairs, share, LANES).astype(jnp.bfloat16)
         )
@@ -283,7 +283,19 @@
             device_id_type=MESH,
         )
 
+    def turn_to_gate(i, _):
+        here = pl.ds(pl.multiple_of(i * cols, cols), cols)
+        normed[here, :] = jax.nn.sigmoid(
+            jnp.dot(
+                normed[here, :].astype(jnp.bfloat16),
+                w_gate[...],
+                preferred_element_type=jnp.float32,
+            )
+        )
+        return 0
+
     def finish_own():
+        lax.fori_loop(0, rows, turn_to_gate, 0, unroll=4)
         locals_[1].wait()
         for copy in trades[1]:
             copy.wait()
@@ -394,17 +406,11 @@
         )
         for part in range(2):
             i = part * pairs + t
-            gate = jax.nn.sigmoid(
-                jnp.dot(
-                    normed[pl.ds(pl.multiple_of(i * cols, cols), cols), :].astype(jnp.bfloat16),
-                    w_gate[...],
-                    preferred_element_type=jnp.float32,
-                )
-            )
+            gate = normed[pl.ds(pl.multiple_of(i * cols, cols), cols), :]
             out[i] = (state[i] + gate * update[part * half : (part + 1) * half]).astype(out.dtype)
         return 0
 
-    lax.fori_loop(0, pairs, finish, 0, unroll=2)
+    lax.fori_loop(0, pairs, finish, 0, unroll=4)
 
 
 def fused_update(

time: 254 us -> 247 us (0.972)
  Pallas kernels: 221 us -> 215 us
    pallas_call x2, Pallas kernels: 187 us -> 180 us  [fused_update(): pl.pallas_call(functools.partial(triangle_kernel, incoming), out_shape=ja...]
where the time goes in v5:
time: 247 us
  Pallas kernels  215 us (87%)
  matrix products  12.7 us (5%)
  local copies, waits for them, and re-layouts  10.4 us (4%)
  other arithmetic  7.64 us (3%)
    pallas_call x2, Pallas kernels, fused_update(): pl.pallas_call(functools.partial(triangle_kernel, incoming), out_shape=ja...  180 us
    pallas_call x1, Pallas kernels, fused_attention(): pl.pallas_call(functools.partial(attention_kernel, heads), out_shape=jax....  23.3 us
    pallas_call x1, Pallas kernels, trade_factors(): pl.pallas_call(factor_kernel, out_shape=[jax.ShapeDtypeStruct(shape, jnp....  11.3 us
    dot_general x1, matrix products, body(): jnp.einsum('sic,scjz->ijz', left_rows, spread_right, preferred_element_ty...  8.76 us

profile of v5, /device:TPU:0, one launch (start us, length us, event | category | flops | bytes accessed | tf_op | source)
XLA Modules:
  0.0 247.0 jit_solution(13416056334007186646)
XLA Ops:
  0.7 0.9 fusion.50
  1.6 2.4 fusion.52
  4.0 1.3 multiply_reduce_fusion
  5.4 1.3 multiply_convert_fusion
  6.8 0.4 fusion.42
  7.2 0.4 copy-done.4
  7.6 0.1 convert_reduce_fusion
  7.8 0.3 fusion.18
  8.1 0.5 fusion.29
  8.8 23.3 %attention.1 = f32[8,64,256]{2,1,0:T(8,128)S(1)} custom-call(bf16[8,64,256]{2,1,0:T(8,128)(2,1)S(1)} %fusion.24.query, bf16[8,64,512]{2,1,0:T(8,128)(2,1)S(1)} %slice.126.own_kv, bf16[8,32,128]{2,1,0:T(8,128)(2,1)S(1)} %bitcast.84, f32[8,128]{1,0:T(8,128)S(1)} %pad.4.own_mask), custom_call_target="tpu_custom_call" | custom-call | flops 1073741824 | bytes 4194304 | tf_op jit(solution)/shard_map/attention/pallas_call | solution.py:611
  32.1 0.4 convert_reduce_fusion.1
  32.5 0.3 fusion.21
  32.8 0.2 fusion.23
  33.1 0.2 fusion.12
  33.3 0.6 pad_maximum_fusion
  34.0 11.3 %factors.1 = (bf16[4,48,512]{2,1,0:T(8,128)(2,1)}, bf16[4,48,512]{2,1,0:T(8,128)(2,1)}) custom-call(bf16[48,512]{1,0:T(8,128)(2,1)} %get-tuple-element.21.left, bf16[48,512]{1,0:T(8,128)(2,1)} %get-tuple-element.20.right), custom_call_target="tpu_custom_call" | custom-call | bytes 1048576 | tf_op jit(solution)/shard_map/factors/pallas_call | solution.py:711
  45.3 0.9 slice_reduce_fusion.1
  46.2 0.8 slice_reduce_fusion
  47.1 0.2 convolution_add_fusion.1
  47.3 0.9 slice.76
  48.2 0.2 reshape.151
  48.4 0.8 copy.54
  49.3 0.2 reshape.149
  49.5 8.8 %fusion.7 = f32[64,64,128]{2,0,1:T(8,128)} fusion(bf16[32,64,32,1]{2,0,3,1:T(8,128)(2,1)S(1)} %copy.54, bf16[32,32,128,1]{2,1,0,3:T(8,128)(2,1)S(1)} %bitcast.93, bf16[4,32,8,64]{3,2,1,0:T(8,128)(2,1)S(1)} %reshape.149), kind=kOutput, calls=%fused_computation.11 | convolution fusion | flops 1619001344 | bytes 2621440 | tf_op jit(solution)/shard_map/sic,scjz->ijz/dot_general | solution.py:907
  58.3 3.4 %fusion.5.state = f32[64,64,128]{2,1,0:T(8,128)S(1)} fusion(f32[64,64,128]{2,1,0:T(8,128)} %copy-done.3, f32[64,64,128]{2,0,1:T(8,128)} %fusion.7, f32[64,64]{1,0:T(8,128)S(1)} %convolution_add_fusion.1), kind=kLoop, calls=%fused_computation.5 | loop fusion | flops 1048576 | bytes 6307840 | tf_op jit(solution)/shard_map/add | solution.py:944
  61.7 0.1 copy.58
  62.2 75.9 %triangle_out.1.state = f32[64,64,128]{2,1,0:T(8,128)S(1)} custom-call(f32[64,64,128]{2,1,0:T(8,128)S(1)} %fusion.5.state, f32[32,1,128]{2,1,0:T(1,128)S(1)} %reshape.155.flags, f32[1,128]{1,0:T(1,128)S(1)} %get-tuple-element.25.norm_gain, bf16[256,128]{1,0:T(8,128)(2,1)S(1)} %get-tuple-element.11.w_own, bf16[256,128]{1,0:T(8,128)(2,1)S(1)} %get-tuple-element.10.w_spread, ...), custom_call_target="tpu_custom_call" | custom-call | flops 268435456 | bytes 8388608 | tf_op jit(solution)/shard_map/triangle_out/pallas_call | solution.py:432
  138.1 1.3 copy-done.1
  139.4 0.1 copy.59
  139.9 1.6 copy-done.2
  141.4 104.6 %triangle_in.1 = bf16[64,64,128]{2,1,0:T(8,128)(2,1)S(1)} custom-call(f32[64,64,128]{2,1,0:T(8,128)S(1)} %copy-done.2, f32[32,1,128]{2,1,0:T(1,128)S(1)} %reshape.157.flags, f32[1,128]{1,0:T(1,128)S(1)} %get-tuple-element.24.norm_gain, bf16[256,128]{1,0:T(8,128)(2,1)S(1)} %get-tuple-element.9.w_own, bf16[256,128]{1,0:T(8,128)(2,1)S(1)} %get-tuple-element.8.w_spread, ...), custom_call_target="tpu_custom_call" | custom-call | flops 268435456 | bytes 8388608 | tf_op jit(solution)/shard_map/triangle_in/pallas_call | solution.py:432
  246.0 1.0 copy.72
  (74 shorter events, 1.5 us)
Async XLA Ops:
  0.6 7.4 %copy-start = (bf16[256,1024]{1,0:T(8,128)(2,1)S(1)}, bf16[256,1024]{1,0:T(8,128)(2,1)}, u32[]{:S(2)}) copy-start(bf16[256,1024]{1,0:T(8,128)(2,1)} %param.30) | copy-start | bytes 1572868
  1.6 3.8 %copy-start.18 = (f32[128]{0:T(128)S(1)}, f32[128]{0:T(128)}, u32[]{:S(2)}) copy-start(f32[128]{0:T(128)} %param.27) | copy-start | bytes 1540
  4.0 2.7 %copy-start.3 = (f32[64,64,128]{2,1,0:T(8,128)}, f32[64,64,128]{2,1,0:T(8,128)S(1)}, u32[]{:S(2)}) copy-start(f32[64,64,128]{2,1,0:T(8,128)S(1)} %get-tuple-element.31) | copy-start | bytes 6291460
  5.4 1.4 copy-start.13
  6.7 1.0 copy-start.4
  6.7 1.4 copy-start.14
  8.1 0.7 copy-start.12
  8.8 23.3 %copy-start.20 = (bf16[256,256]{1,0:T(8,128)(2,1)S(1)}, bf16[256,256]{1,0:T(8,128)(2,1)}, u32[]{:S(2)}) copy-start(bf16[256,256]{1,0:T(8,128)(2,1)} %param.31) | copy-start | bytes 393220
  32.1 0.7 copy-start.15
  32.1 1.0 copy-start.11
  32.5 17.0 %copy-start.5 = (bf16[8,64,256]{2,1,0:T(8,128)(2,1)}, bf16[8,64,256]{2,1,0:T(8,128)(2,1)S(1)}, u32[]{:S(2)}) copy-start(bf16[8,64,256]{2,1,0:T(8,128)(2,1)S(1)} %get-tuple-element.40) | copy-start | bytes 786436
  32.8 16.7 %copy-start.19 = (bf16[1024,128]{1,0:T(8,128)(2,1)S(1)}, bf16[1024,128]{1,0:T(8,128)(2,1)}, u32[]{:S(2)}) copy-start(bf16[1024,128]{1,0:T(8,128)(2,1)} %param.34) | copy-start | bytes 786436
  45.3 4.0 %copy-start.7 = (bf16[4,48,512]{2,1,0:T(8,128)(2,1)S(1)}, bf16[4,48,512]{2,1,0:T(8,128)(2,1)}, u32[]{:S(2)}) copy-start(bf16[4,48,512]{2,1,0:T(8,128)(2,1)} %get-tuple-element.4) | copy-start | bytes 589828
  58.2 3.4 %copy-start.8 = (bf16[2,128,128]{2,1,0:T(8,128)(2,1)S(1)}, bf16[2,128,128]{2,1,0:T(8,128)(2,1)}, u32[]{:S(2)}) copy-start(bf16[2,128,128]{2,1,0:T(8,128)(2,1)} %param.39) | copy-start | bytes 196612
  58.2 3.4 %copy-start.9 = (bf16[2,128,128]{2,1,0:T(8,128)(2,1)S(1)}, bf16[2,128,128]{2,1,0:T(8,128)(2,1)}, u32[]{:S(2)}) copy-start(bf16[2,128,128]{2,1,0:T(8,128)(2,1)} %param.37) | copy-start | bytes 196612
  58.2 3.4 %copy-start.6 = (bf16[2,128,512]{2,1,0:T(8,128)(2,1)S(1)}, bf16[2,128,512]{2,1,0:T(8,128)(2,1)}, u32[]{:S(2)}) copy-start(bf16[2,128,512]{2,1,0:T(8,128)(2,1)} %param.36) | copy-start | bytes 786436
  58.2 3.6 %copy-start.10 = (s32[64,64]{1,0:T(8,128)S(1)}, s32[64,64]{1,0:T(8,128)}, u32[]{:S(2)}) copy-start(s32[64,64]{1,0:T(8,128)} %param.23) | copy-start | bytes 49156
  58.2 3.8 %copy-start.16 = (f32[2,128]{1,0:T(2,128)S(1)}, f32[2,128]{1,0:T(2,128)}, u32[]{:S(2)}) copy-start(f32[2,128]{1,0:T(2,128)} %param.38) | copy-start | bytes 3076
  58.2 3.9 %copy-start.17 = (f32[2,128]{1,0:T(2,128)S(1)}, f32[2,128]{1,0:T(2,128)}, u32[]{:S(2)}) copy-start(f32[2,128]{1,0:T(2,128)} %param.35) | copy-start | bytes 3076
  138.0 1.3 copy-start.1
  139.9 1.6 copy-start.2
